TPU v7x, 32 devices: a whole 2x2x4 slice. The times are simulated.
32 devices in a mesh: rep: 8 (over y, x, core), shard: 4 (over z).
Axes of the slice: x: 2, y: 2, z: 4, core: 2. Of those that a mesh axis runs over, the one named last changes fastest.
Arguments:
- tokens: bfloat16 [8192, 2048], P(('rep', 'shard')), may hold values from -6 to 6
- cotangent: bfloat16 [8192, 2048], P(('rep', 'shard')), may hold values from -6 to 6
- live_counts: int32 [8, 4], P('rep'), may hold values from 128 to 256, as said below
- routes: int32 [8192, 2], P(('rep', 'shard')), may hold values from 0 to 3, all different within a row
- norm_in: bfloat16 [2048], P('shard'), may hold values from 0.5 to 1.5
- w_query: bfloat16 [2048, 2048], P('shard'), may hold values from -0.125 to 0.125
- w_key: bfloat16 [2048, 2048], P('shard'), may hold values from -0.125 to 0.125
- w_value: bfloat16 [2048, 2048], P('shard'), may hold values from -0.125 to 0.125
- norm_query: bfloat16 [2048], P('shard'), may hold values from 0.5 to 1.5
- norm_key: bfloat16 [2048], P('shard'), may hold values from 0.5 to 1.5
- w_out: bfloat16 [2048, 2048], P('shard'), may hold values from -1 to 1
- norm_mid: bfloat16 [2048], P('shard'), may hold values from 0.5 to 1.5
- w_router: bfloat16 [2048, 4], P('shard'), may hold values from -0.09375 to 0.09375
- w_gate: bfloat16 [4, 2048, 1024], P(None, 'shard'), may hold values from -0.125 to 0.125
- w_up: bfloat16 [4, 2048, 1024], P(None, 'shard'), may hold values from -0.125 to 0.125
- w_down: bfloat16 [4, 1024, 2048], P(None, 'shard'), may hold values from -0.5 to 0.5
Outputs:
- output: bfloat16 [8192, 2048], P(('rep', 'shard'))
- input_grad: bfloat16 [8192, 2048], P(('rep', 'shard'))
- norm_in_grad: float32 [2048], P('shard')
- w_query_grad: float32 [2048, 2048], P('shard')
- w_key_grad: float32 [2048, 2048], P('shard')
- w_value_grad: float32 [2048, 2048], P('shard')
- norm_query_grad: float32 [2048], P('shard')
- norm_key_grad: float32 [2048], P('shard')
- w_out_grad: float32 [2048, 2048], P('shard')
- norm_mid_grad: float32 [2048], P('shard')
- w_router_grad: float32 [2048, 4], P('shard')
- w_gate_grad: float32 [4, 2048, 1024], P(None, 'shard')
- w_up_grad: float32 [4, 2048, 1024], P(None, 'shard')
- w_down_grad: float32 [4, 1024, 2048], P(None, 'shard')
Inputs may be any that keep to these rules, and one draw needn't show every extreme that they name: Of a device's 256 rows, the first live_counts of them are live and the rest are unused; some device holds exactly 256 live rows and some exactly 128.
All inputs are finite; a program needn't handle non-finite values.
Results may differ from a plain program's by a relative error of at most 0.024.
Values may be sent and summed in bfloat16 or wider, within the bound.
No kernel may reach another device: no remote copies, remote signals or barrier semaphores. Data moves between devices by JAX's collectives and lax.ppermute only.
A program may use at most 512 MiB of HBM per device.

v0:
```python
import functools

import jax
import jax.numpy as jnp
from jax import lax
from jax.experimental import pallas as pl
from jax.experimental.pallas import tpu as pltpu
from jax.sharding import Mesh
from jax.sharding import PartitionSpec as P

HEADS = 16
EPS = 1e-05
THETA = 10000.0
MASKED = -1e30
FAR = 1 << 30
F32 = jnp.float32
BF16 = jnp.bfloat16
VMEM_BYTES = 56 * 1024 * 1024


def dot(left, right):
    return jnp.dot(left, right, preferred_element_type=F32)


def dot_nt(left, right):
    return lax.dot_general(left, right, (((1,), (1,)), ((), ())), preferred_element_type=F32)


def dot_tn(left, right):
    return lax.dot_general(left, right, (((0,), (0,)), ((), ())), preferred_element_type=F32)


def tie(*values):
    return lax.optimization_barrier(values)


def tie_lists(*lists):
    return lax.optimization_barrier([list(values) for values in lists])


def swap(value, axis, step):
    size = lax.axis_size(axis)
    return lax.ppermute(value, axis, [(i, i ^ step) for i in range(size)])


def exchange(parts, axis):
    me = lax.axis_index(axis)
    out = parts
    for step in range(1, lax.axis_size(axis)):
        sent = lax.dynamic_index_in_dim(parts, me ^ step, 0, keepdims=True)
        out = lax.dynamic_update_slice_in_dim(out, swap(sent, axis, step), me ^ step, 0)
    return out


def gather_first(block):
    chips = lax.axis_size("chip")
    if chips != 4:
        return [block] + [swap(block, "chip", step) for step in range(1, chips)]
    half = block.shape[0] // 2
    top, low = block[:half], block[half:]
    two_top, one_low = swap(top, "chip", 2), swap(low, "chip", 1)
    one_top, two_low = swap(top, "chip", 1), swap(low, "chip", 2)
    return [block, one_top, one_low, two_top, two_low]


def gather_last(pieces):
    if lax.axis_size("chip") != 4:
        return pieces
    return pieces + [swap(pieces[3], "chip", 1), swap(pieces[2], "chip", 2)]


def scatter_first(split):
    if len(split) == 2:
        return split
    own_left, own_right, to_one, to_two, keep_left, keep_right = split
    return (own_left, own_right, swap(to_one, "chip", 1), swap(to_two, "chip", 2), keep_left, keep_right)


def scatter_pass(first):
    if len(first) == 2:
        return (first[1][0],)
    _, _, from_one, from_two, keep_left, keep_right = first
    return (
        (keep_left.astype(F32) + from_one[1].astype(F32)).astype(BF16),
        (keep_right.astype(F32) + from_two[1].astype(F32)).astype(BF16),
    )


def scatter_second(passed):
    if len(passed) == 1:
        return list(passed)
    return [swap(passed[0], "chip", 2), swap(passed[1], "chip", 1)]


def scatter_sum(first, arrived):
    if len(first) == 2:
        own, others = first
        for step, other in enumerate(tuple(arrived) + tuple(others[1:])):
            own = own + swap(other, "chip", step + 1).astype(F32)
        return own
    own_left, own_right, from_one, from_two, _, _ = first
    return jnp.concatenate(
        [
            own_left + from_one[0].astype(F32) + arrived[0].astype(F32),
            own_right + from_two[0].astype(F32) + arrived[1].astype(F32),
        ],
        axis=1,
    )


def scatter_chips(split):
    first = scatter_first(split)
    return scatter_sum(first, scatter_second(scatter_pass(first)))


def sum_chips(value):
    step = 1
    while step < lax.axis_size("chip"):
        value = value + swap(value, "chip", step)
        step *= 2
    return value


def sum_rows(values):
    chips = lax.axis_size("chip")
    total = values.reshape(values.shape[0], chips, -1)
    step = 1
    while step < chips:
        other = swap(total, "chip", step)
        total = total + jnp.concatenate([other[:, i ^ step : (i ^ step) + 1] for i in range(chips)], axis=1)
        step *= 2
    return total.reshape(values.shape)


def rehome_chips(rows):
    chips = lax.axis_size("chip")
    parts = rows.reshape(chips, rows.shape[0] // chips, rows.shape[1])
    return lax.all_to_all(parts, "chip", 0, 0, tiled=True)


def rehome_planes(parts):
    return lax.all_to_all(parts, "shard", 0, 0, tiled=True).reshape(-1, parts.shape[2])


def home_planes(rows):
    shards = lax.axis_size("shard")
    parts = rows.reshape(shards, rows.shape[0] // shards, rows.shape[1])
    return lax.all_to_all(parts, "shard", 0, 0, tiled=True)


def home_chips(parts):
    return lax.all_to_all(parts, "chip", 0, 0, tiled=True).reshape(-1, parts.shape[2])


ANYWHERE = pl.BlockSpec(memory_space=pl.ANY)


def run(kernel, name, micros, grid, in_specs, out_specs, out_shape, args, scratch=()):
    return pl.pallas_call(
        kernel,
        grid=grid,
        in_specs=in_specs,
        out_specs=out_specs,
        out_shape=out_shape,
        scratch_shapes=list(scratch),
        compiler_params=pltpu.CompilerParams(vmem_limit_bytes=VMEM_BYTES),
        cost_estimate=pl.CostEstimate(flops=micros * 550_000_000, bytes_accessed=1024, transcendentals=0),
        name=name,
    )(*args)


def load_rows(pieces, target, sems):
    copies, at = [], 0
    for i, piece in enumerate(pieces):
        copies.append(pltpu.make_async_copy(piece, target.at[pl.ds(at, piece.shape[0]), :], sems.at[i]))
        at += piece.shape[0]
    for copy in copies:
        copy.start()
    for copy in copies:
        copy.wait()


def rows_scratch(pieces):
    rows = sum(piece.shape[0] for piece in pieces)
    return [pltpu.VMEM((rows, pieces[0].shape[1]), BF16), pltpu.SemaphoreType.DMA((len(pieces),))]


def column_sums(values):
    ones = jnp.ones((8, values.shape[1]), F32)
    return lax.dot_general(
        ones, values, (((1,), (1,)), ((), ())), precision=lax.Precision.HIGHEST, preferred_element_type=F32
    )


def project_kernel(count, *refs):
    pieces, (weight, out, squares, rows, sems) = refs[:count], refs[count:]

    @pl.when(pl.program_id(0) == 0)
    def _():
        load_rows(pieces, rows, sems)

    result = dot(rows[...], weight[...])
    out[...] = result
    squares[...] = column_sums(result * result)


def run_project(pieces, weight, tile):
    depth, columns = weight.shape
    rows = sum(piece.shape[0] for piece in pieces)
    steps = columns // tile
    return run(
        functools.partial(project_kernel, len(pieces)), "project", 16, (steps,),
        [ANYWHERE] * len(pieces) + [pl.BlockSpec((depth, tile), lambda i: (0, i))],
        [pl.BlockSpec((rows, tile), lambda i: (0, i)), pl.BlockSpec((8, rows), lambda i: (i, 0))],
        [jax.ShapeDtypeStruct((rows, columns), F32), jax.ShapeDtypeStruct((8 * steps, rows), F32)],
        (*pieces, weight),
        rows_scratch(pieces),
    )


def back_kernel(count, *refs):
    pieces, (weight, out, rows, sems) = refs[:count], refs[count:]

    @pl.when(pl.program_id(0) == 0)
    def _():
        load_rows(pieces, rows, sems)

    out[...] = dot_nt(rows[...], weight[...]).astype(BF16)


def run_back(pieces, weight, tile):
    rows = sum(piece.shape[0] for piece in pieces)
    return run(
        functools.partial(back_kernel, len(pieces)), "back", 7, (weight.shape[0] // tile,),
        [ANYWHERE] * len(pieces) + [pl.BlockSpec((tile, weight.shape[1]), lambda i: (i, 0))],
        pl.BlockSpec((rows, tile), lambda i: (0, i)),
        jax.ShapeDtypeStruct((rows, weight.shape[0]), BF16),
        (*pieces, weight),
        rows_scratch(pieces),
    )


def join_experts(ref):
    parts, experts, units, columns = ref.shape
    if parts == 1:
        return ref[...].reshape(experts * units, columns)
    return jnp.concatenate([ref[:, expert].reshape(parts * units, columns) for expert in range(experts)], axis=0)


def split_kernel(block, turned, left, left_w, right_w, own_left, own_right, to_one, to_two, keep_left, keep_right):
    def product(weight):
        if turned:
            return dot_nt(left[...], weight[...])
        return dot(left[...], weight[...] if len(weight.shape) == 2 else join_experts(weight))

    result = product(left_w)
    own_left[...] = result[:block]
    to_one[0] = result[block : 2 * block].astype(BF16)
    keep_left[...] = result[2 * block : 3 * block].astype(BF16)
    to_one[1] = result[3 * block :].astype(BF16)
    result = product(right_w)
    own_right[...] = result[:block]
    keep_right[...] = result[block : 2 * block].astype(BF16)
    to_two[0] = result[2 * block : 3 * block].astype(BF16)
    to_two[1] = result[3 * block :].astype(BF16)


def split_matmul(left, weight, turned, micros):
    chips = lax.axis_size("chip")
    rows = left.shape[0]
    block = rows // chips
    width = weight.shape[0] if turned else weight.shape[-1]
    if chips != 4:
        if weight.ndim == 4:
            weight = weight.transpose(1, 0, 2, 3).reshape(-1, width)
        whole = (dot_nt if turned else dot)(left, weight)
        return (whole[:block], [whole[i * block : (i + 1) * block].astype(BF16) for i in range(1, chips)])
    half, tile = width // 2, 256
    steps = half // tile

    def weight_spec(first):
        if turned:
            return pl.BlockSpec((tile, weight.shape[1]), lambda i: (first + i, 0))
        return pl.BlockSpec((*weight.shape[:-1], tile), lambda i: (0,) * (weight.ndim - 1) + (first + i,))

    one = pl.BlockSpec((block, tile), lambda i: (0, i))
    two = pl.BlockSpec((2, block, tile), lambda i: (0, 0, i))
    wide, low = jax.ShapeDtypeStruct((block, half), F32), jax.ShapeDtypeStruct((block, half), BF16)
    pair = jax.ShapeDtypeStruct((2, block, half), BF16)
    return run(
        functools.partial(split_kernel, block, turned), "split_matmul", micros, (steps,),
        [pl.BlockSpec(left.shape, lambda i: (0, 0)), weight_spec(0), weight_spec(steps)],
        [one, one, two, two, one, one],
        [wide, wide, pair, pair, low, low],
        (left, weight, weight),
    )


def weight_grad_kernel(count, tile, *refs):
    pieces, (grad, out, rows, sems) = refs[:count], refs[count:]

    @pl.when(pl.program_id(0) == 0)
    def _():
        load_rows(pieces, rows, sems)

    columns = pl.ds(pl.multiple_of(pl.program_id(0) * tile, tile), tile)
    out[...] = dot_tn(rows[:, columns], grad[...]).astype(BF16)


def run_weight_grad(pieces, grad, micros, columns=None):
    tile = 512
    depth, columns = pieces[0].shape[1], columns or grad.shape[1]
    return run(
        functools.partial(weight_grad_kernel, len(pieces), tile), "weight_grad", micros, (depth // tile,),
        [ANYWHERE] * len(pieces) + [pl.BlockSpec((grad.shape[0], columns), lambda i: (0, 0))],
        pl.BlockSpec((tile, columns), lambda i: (i, 0)),
        jax.ShapeDtypeStruct((depth, columns), BF16),
        (*pieces, grad),
        rows_scratch(pieces),
    )


def down_grad_kernel(experts, parts, act, upstream, out):
    result = dot_tn(act[...], upstream[...]).astype(BF16)
    own = result.shape[0] // (experts * parts)
    for expert in range(experts):
        for part in range(parts):
            at = (expert * parts + part) * own
            out[part, expert * own : (expert + 1) * own, :] = result[at : at + own]


def run_down_grad(act, upstream, width, experts, parts):
    hidden, tile = act.shape[1], 512
    return run(
        functools.partial(down_grad_kernel, experts, parts), "down_grad", 9, (width // tile,),
        [pl.BlockSpec(act.shape, lambda i: (0, 0)), pl.BlockSpec((upstream.shape[0], tile), lambda i: (0, i))],
        pl.BlockSpec((parts, hidden // parts, tile), lambda i: (0, 0, i)),
        jax.ShapeDtypeStruct((parts, hidden // parts, width), BF16),
        (act, upstream),
    )


def out_grad_kernel(count, tile, *refs):
    pieces, (mixed, out, rows, sems) = refs[:count], refs[count:]

    @pl.when(pl.program_id(0) == 0)
    def _():
        load_rows(pieces, rows, sems)

    columns = pl.ds(pl.multiple_of(pl.program_id(0) * tile, tile), tile)
    out[...] = dot_tn(mixed[...], rows[:, columns]).astype(BF16)


def run_out_grad(mixed, pieces):
    tile, width = 512, pieces[0].shape[1]
    return run(
        functools.partial(out_grad_kernel, len(pieces), tile), "out_grad", 7, (width // tile,),
        [ANYWHERE] * len(pieces) + [pl.BlockSpec(mixed.shape, lambda i: (0, 0))],
        pl.BlockSpec((mixed.shape[1], tile), lambda i: (0, i)),
        jax.ShapeDtypeStruct((mixed.shape[1], width), BF16),
        (*pieces, mixed),
        rows_scratch(pieces),
    )


def lane_roll(values):
    return pltpu.roll(values, values.shape[1] // 2, 1)


def take_block(ref, block, chips, block_rows):
    piece = block_rows // chips
    at = lambda chip: chip * block_rows + block * piece
    return jnp.concatenate([ref[at(chip) : at(chip) + piece, :] for chip in range(chips)], axis=0)


def put_block(ref, block, chips, block_rows, values):
    piece = block_rows // chips
    for chip in range(chips):
        at = chip * block_rows + block * piece
        ref[at : at + piece, :] = values[chip * piece : (chip + 1) * piece]


def attend_forward(
    chips, block_rows, scale,
    query_ref, key_ref, value_ref, inv_ref, gain_q, gain_k, cos_ref, sin_ref, pos_ref, key_pos_ref,
    mixed, query_rot, key_rot, value_low, lse,
):
    blocks = inv_ref.shape[0] // block_rows
    for block in range(blocks):
        rows = pl.ds(block * block_rows, block_rows)
        cosine, sine = cos_ref[rows, :], sin_ref[rows, :]
        inv = take_block(inv_ref, block, chips, block_rows)
        query = take_block(query_ref, block, chips, block_rows) * inv[:, 0:1] * gain_q[...]
        query_rot[rows, :] = (query * cosine + lane_roll(query) * sine).astype(BF16)
        key = take_block(key_ref, block, chips, block_rows) * inv[:, 1:2] * gain_k[...]
        key_rot[rows, :] = (key * cosine + lane_roll(key) * sine).astype(BF16)
        value_low[rows, :] = take_block(value_ref, block, chips, block_rows).astype(BF16)
    for block in range(blocks):
        rows = pl.ds(block * block_rows, block_rows)
        seen = pl.ds(0, (block + 1) * block_rows)
        scores = dot_nt(query_rot[rows, :], key_rot[seen, :]) * scale
        scores = jnp.where(key_pos_ref[:, seen] <= pos_ref[rows, :], scores, MASKED)
        peak = jnp.max(scores, axis=-1, keepdims=True)
        expo = jnp.exp(scores - peak)
        total = jnp.sum(expo, axis=-1, keepdims=True)
        probs_low = (expo * (1.0 / total)).astype(BF16)
        put_block(mixed, block, chips, block_rows, dot(probs_low, value_low[seen, :]).astype(BF16))
        lse[rows, :] = jnp.broadcast_to(peak + jnp.log(total), (block_rows, lse.shape[1]))


def attend_backward(
    chips, block_rows, scale,
    grad_ref, query_ref, key_ref, query_rot, key_rot, value_low, lse, gain_q, gain_k,
    inv_ref, cos_ref, sin_ref, pos_ref, key_pos_ref,
    query_back, key_back, value_back, gains, sums_ref,
    key_sum, value_sum,
):
    blocks = inv_ref.shape[0] // block_rows

    @pl.when(pl.program_id(0) == 0)
    def _():
        sums_ref[...] = jnp.zeros_like(sums_ref)

    key_sum[...] = jnp.zeros_like(key_sum)
    value_sum[...] = jnp.zeros_like(value_sum)
    for block in range(blocks):
        rows = pl.ds(block * block_rows, block_rows)
        seen = pl.ds(0, (block + 1) * block_rows)
        query = query_rot[rows, :]
        grad = take_block(grad_ref, block, chips, block_rows)
        scores = dot_nt(query, key_rot[seen, :]) * scale
        scores = jnp.where(key_pos_ref[:, seen] <= pos_ref[rows, :], scores, MASKED)
        probs = jnp.exp(scores - lse[rows, 0:1])
        probs_grad = dot_nt(grad, value_low[seen, :])
        weighted = jnp.sum(probs * probs_grad, axis=-1, keepdims=True)
        score_grad = (probs * (probs_grad - weighted)).astype(BF16)
        query_grad = dot(score_grad, key_rot[seen, :]) * scale
        turned = query_grad * cos_ref[rows, :] - lane_roll(query_grad) * sin_ref[rows, :]
        put_block(query_back, block, chips, block_rows, turned)
        key_sum[seen, :] += dot_tn(score_grad, query)
        value_sum[seen, :] += dot_tn(probs.astype(BF16), grad)
    for block in range(blocks):
        rows = pl.ds(block * block_rows, block_rows)
        key_grad = key_sum[rows, :] * scale
        turned = key_grad * cos_ref[rows, :] - lane_roll(key_grad) * sin_ref[rows, :]
        put_block(key_back, block, chips, block_rows, turned)
        put_block(value_back, block, chips, block_rows, value_sum[rows, :].astype(BF16))
    for which, (lin, back, gain) in enumerate(((query_ref, query_back, gain_q), (key_ref, key_back, gain_k))):
        product = back[...] * lin[...] * inv_ref[:, which : which + 1]
        sums_ref[pl.ds(8 * which, 8), :] += column_sums(product * gain[...])
        gains[pl.ds(8 * which, 8), :] = jnp.broadcast_to(jnp.sum(product, axis=0, keepdims=True), (8, product.shape[1]))


def attention_specs(rows, head_size, heads):
    column = pl.BlockSpec((rows, head_size), lambda h: (0, h))
    whole = lambda shape: pl.BlockSpec(shape, lambda h: (0, 0))
    part = [pl.BlockSpec((rows, head_size), lambda h, which=which: (0, which * heads + h)) for which in range(3)]
    gain = pl.BlockSpec((1, head_size), lambda h: (0, h))
    return column, whole, part, gain


def run_attend_forward(lin, inv, gains, angles, chips, heads, head_size, block_rows):
    rows, wide = lin.shape[0], heads * head_size
    column, whole, part, gain = attention_specs(rows, head_size, heads)
    low = jax.ShapeDtypeStruct((rows, wide), BF16)
    return run(
        functools.partial(attend_forward, chips, block_rows, head_size**-0.5), "attend_forward", 17, (heads,),
        part + [whole(inv.shape), gain, gain] + [whole(v.shape) for v in angles],
        [column] * 5,
        [low, low, low, low, jax.ShapeDtypeStruct((rows, wide), F32)],
        (lin, lin, lin, inv, *gains, *angles),
    )


def run_attend_backward(mixed_grad, lin, kept, inv, gains, angles, chips, heads, head_size, block_rows):
    rows, wide = mixed_grad.shape
    column, whole, part, gain = attention_specs(rows, head_size, heads)
    full = jax.ShapeDtypeStruct((rows, wide), F32)
    return run(
        functools.partial(attend_backward, chips, block_rows, head_size**-0.5), "attend_backward", 20, (heads,),
        [column, part[0], part[1]] + [column] * 4 + [gain, gain, whole(inv.shape)] + [whole(v.shape) for v in angles],
        [column] * 3 + [pl.BlockSpec((16, head_size), lambda h: (0, h)), whole((16, rows))],
        [full, full, jax.ShapeDtypeStruct((rows, wide), BF16), jax.ShapeDtypeStruct((16, wide), F32),
         jax.ShapeDtypeStruct((16, rows), F32)],
        (mixed_grad, lin, lin, *kept, *gains, inv, *angles),
        [pltpu.VMEM((rows, head_size), F32)] * 2,
    )


def finish_kernel(wide, query_back, key_back, value_back, lin, gain_q, gain_k, inv_ref, mean_ref, out):
    for which, (back, gain) in enumerate(((query_back, gain_q), (key_back, gain_k))):
        inv = inv_ref[:, which : which + 1]
        columns = slice(which * wide, (which + 1) * wide)
        unit = lin[:, columns] * inv
        out[:, columns] = (inv * (gain[...] * back[...] - unit * mean_ref[:, which : which + 1])).astype(BF16)
    out[:, 2 * wide :] = value_back[...]


def run_finish(backs, lin, gains, inv, means, tile):
    rows, wide = backs[0].shape
    spec = lambda columns: pl.BlockSpec((tile, columns), lambda i: (i, 0))
    gain = pl.BlockSpec((1, wide), lambda i: (0, 0))
    return run(
        functools.partial(finish_kernel, wide), "finish", 7, (rows // tile,),
        [spec(wide)] * 3 + [spec(3 * wide), gain, gain, spec(2), spec(2)],
        spec(3 * wide),
        jax.ShapeDtypeStruct((rows, 3 * wide), BF16),
        (*backs, lin, *gains, inv, means),
    )


def experts_kernel(count, experts, top, *refs):
    middles, upstreams, refs = refs[:count], refs[count : 2 * count], refs[2 * count :]
    gate_w, up_w, down_w, router_w, act_out, grad_out, mix_grad, middle, upstream, mix, middle_sems, upstream_sems = refs
    step, tile = pl.program_id(0), gate_w.shape[1]
    rows, depth = middle.shape
    lane = lax.broadcasted_iota(jnp.int32, (1, mix.shape[1]), 1)

    @pl.when(step == 0)
    def _():
        load_rows(middles, middle, middle_sems)
        load_rows(upstreams, upstream, upstream_sems)
        mix_grad[...] = jnp.zeros_like(mix_grad)
        logits = jnp.where(lane < experts, dot_nt(middle[...], router_w[...]), MASKED)
        expo = jnp.exp(logits - jnp.max(logits, axis=-1, keepdims=True))
        chosen = jnp.zeros_like(expo)
        for i in range(top):
            route = upstream[:, depth + i : depth + i + 1].astype(F32)
            chosen = chosen + jnp.where(route == lane.astype(F32), 1.0, 0.0)
        mix[...] = expo / jnp.sum(expo, axis=-1, keepdims=True) * chosen

    mine = lane == step
    mix_column = jnp.sum(jnp.where(mine, mix[...], 0.0), axis=-1, keepdims=True)
    gate = dot(middle[...], gate_w[...])
    up = dot(middle[...], up_w[...])
    back = dot_nt(upstream[:, :depth], down_w[...].reshape(tile, depth))
    sigma = 1.0 / (1.0 + jnp.exp(-gate))
    silu = gate * sigma
    act = silu * up
    mix_grad[...] += jnp.where(mine, jnp.sum(act * back, axis=-1, keepdims=True), 0.0)
    back = back * mix_column
    act_out[...] = (act * mix_column).astype(BF16)
    columns = pl.ds(pl.multiple_of(step * tile, tile), tile)
    up_columns = pl.ds(pl.multiple_of((experts + step) * tile, tile), tile)
    grad_out[:, columns] = (back * up * sigma * (1.0 + gate * (1.0 - sigma))).astype(BF16)
    grad_out[:, up_columns] = (back * silu).astype(BF16)


def run_experts(middles, upstreams, gate_up, down, router, experts, top):
    rows, depth = sum(piece.shape[0] for piece in middles), middles[0].shape[1]
    parts, _, units, _ = down.shape
    tile = parts * units
    whole = lambda shape: pl.BlockSpec(shape, lambda i: (0, 0))
    grad_shape, mix_shape = (rows, 2 * experts * tile), (rows, router.shape[0])
    buffers, sems = zip(rows_scratch(middles), rows_scratch(upstreams))
    return run(
        functools.partial(experts_kernel, len(middles), experts, top), "experts", 26, (experts,),
        [ANYWHERE] * (2 * len(middles))
        + [
            pl.BlockSpec((depth, tile), lambda i: (0, i)),
            pl.BlockSpec((depth, tile), lambda i: (0, experts + i)),
            pl.BlockSpec((parts, 1, units, depth), lambda i: (0, i, 0, 0)),
            whole(router.shape),
        ],
        [pl.BlockSpec((rows, tile), lambda i: (0, i)), whole(grad_shape), whole(mix_shape)],
        [
            jax.ShapeDtypeStruct((rows, experts * tile), BF16),
            jax.ShapeDtypeStruct(grad_shape, BF16),
            jax.ShapeDtypeStruct(mix_shape, F32),
        ],
        (*middles, *upstreams, gate_up, gate_up, down, router),
        [*buffers, pltpu.VMEM(mix_shape, F32), *sems],
    )


def part_owners(where_ref, chips):
    return [(where_ref[0] ^ step, where_ref[1] ^ turn) for turn in range(2) for step in range(chips)]


def place_heads(chips, heads, head_size, where_ref, *refs):
    parts, outs = refs[: 2 * chips], refs[2 * chips :]
    for part, (chip, core) in zip(parts, part_owners(where_ref, chips)):
        for which, out in enumerate(outs):
            for i in range(heads):
                first = (which * heads + i) * head_size
                column = pl.multiple_of((i * chips + chip) * head_size, head_size)
                out[core, :, pl.ds(column, head_size)] = part[:, first : first + head_size].astype(F32)


def place_hidden(chips, where_ref, *refs):
    count = 2 * chips
    order, outs = refs[2 * count], refs[2 * count + 1 :]
    owners = part_owners(where_ref, chips)
    for which, out in enumerate(outs):
        parts = refs[which * count : (which + 1) * count]
        for turn in range(2):
            row = jnp.concatenate([part[...] for part in parts[turn * chips : (turn + 1) * chips]], axis=1)
            out[0, owners[turn * chips][1]] = dot(row, order[...])


def place_rows(chips, where_ref, *refs):
    parts, out = refs[: 2 * chips], refs[-1]
    height = parts[0].shape[0]
    for part, (chip, core) in zip(parts, part_owners(where_ref, chips)):
        row = pl.multiple_of((2 * chip + core) * height, height)
        out[0, pl.ds(row, height), :] = part[...].astype(F32)


def place(kernel, where, parts, part_blocks, out_shapes, out_block, grid, name, extra=()):
    return pl.pallas_call(
        kernel,
        grid_spec=pltpu.PrefetchScalarGridSpec(
            num_scalar_prefetch=1,
            grid=grid,
            in_specs=[pl.BlockSpec(*block) for block in part_blocks for _ in parts]
            + [pl.BlockSpec(v.shape, lambda i, where: (0, 0)) for v in extra],
            out_specs=[pl.BlockSpec(*out_block)] * len(out_shapes),
        ),
        out_shape=out_shapes,
        compiler_params=pltpu.CompilerParams(vmem_limit_bytes=VMEM_BYTES),
        cost_estimate=pl.CostEstimate(flops=8 * 550_000_000, bytes_accessed=1024, transcendentals=0),
        name=name,
    )(where, *(parts * len(part_blocks)), *extra)


def norm_stats(values):
    inv_root = lax.rsqrt(jnp.mean(values * values, axis=-1, keepdims=True) + EPS)
    return (inv_root, values * inv_root)


def norm_back(gradient, unit_rows, inv_root, gain):
    scaled = gain * gradient
    rows_part = inv_root * (scaled - unit_rows * jnp.mean(unit_rows * scaled, axis=-1, keepdims=True))
    return (rows_part, jnp.sum(gradient * unit_rows, axis=0))


def body(
    tokens, cotangent, live_counts, routes, norm_in, w_query, w_key, w_value, norm_query, norm_key, w_out, norm_mid,
    w_router, w_gate, w_up, w_down,
):
    chips, shards = lax.axis_size("chip"), lax.axis_size("shard")
    chip, core = lax.axis_index("chip"), lax.axis_index("core")
    rows_here, width = tokens.shape
    head_size = width // HEADS
    heads = HEADS // chips
    wide = heads * head_size
    experts, top = w_gate.shape[0], routes.shape[1]
    piece = rows_here // chips
    group_rows = rows_here * shards
    shard_rows = w_query.shape[0]
    half_rows = shard_rows // 2
    shard_hidden, hidden = w_down.shape[1], w_gate.shape[2]
    own_hidden = shard_hidden // (2 * chips)
    parts = 2 * shards
    heads_spread = HEADS // shards == chips
    fast = chips == 4 and own_hidden % 16 == 0 and heads_spread
    where = jnp.stack([chip, core]).astype(jnp.int32)
    owners = ("shard", "core")

    def from_owners(part):
        return lax.all_gather(part, owners, axis=0, tiled=True)

    def to_owners(total):
        return lax.psum_scatter(total, owners, scatter_dimension=0, tiled=True)

    with jax.named_scope("rehome_tokens"):
        token_parts = rehome_chips(tokens)

    head_ids = [i * chips + chip for i in range(heads)]
    with jax.named_scope("weights_qkv"):
        qkv_piece = jnp.concatenate(
            [
                lax.dynamic_slice(w, (core * half_rows, head * head_size), (half_rows, head_size))
                for w in (w_query, w_key, w_value)
                for head in head_ids
            ],
            axis=1,
        )
        qkv_w = from_owners(qkv_piece)
    route_columns = jnp.pad(routes.astype(BF16), ((0, 0), (0, 128 - top)))
    extended = jnp.concatenate([cotangent, route_columns], axis=1)
    small = jnp.concatenate(
        [v.astype(F32)[None] for v in (norm_in, norm_query, norm_key, norm_mid)] + [w_router.astype(F32).T], axis=0
    )
    extended, token_parts = tie(extended, token_parts)
    with jax.named_scope("norm_in"):
        inputs = rehome_planes(token_parts).astype(F32)
    with jax.named_scope("small_gathers"):
        small_all = exchange(jnp.broadcast_to(small[None], (shards,) + small.shape), "shard")
        small_all = small_all.transpose(1, 0, 2).reshape(small.shape[0], width)
        gain_in, gain_query, gain_key, gain_mid = (small_all[i] for i in range(4))
        router = jnp.pad(small_all[4:], ((0, 8 - experts), (0, 0))).astype(BF16)
        counts = lax.ppermute(
            live_counts,
            ("chip", "core", "shard"),
            [
                ((i * 2 + k) * shards + j, (j * 2 + k) * shards + i)
                for i in range(chips)
                for k in range(2)
                for j in range(shards)
            ],
        )[0]
    with jax.named_scope("rehome_cotangent"):
        cotangent_parts = exchange(extended.reshape(chips, piece, extended.shape[1]), "chip")
    hidden_at = 2 * chip * own_hidden
    with jax.named_scope("weights_gate_up"):
        unit = jnp.arange(parts * own_hidden, dtype=jnp.int32)
        wanted = (unit // (2 * own_hidden)) * shard_hidden + hidden_at + unit % (2 * own_hidden)
        choose = (jnp.arange(hidden, dtype=jnp.int32)[:, None] == wanted[None, :]).astype(BF16)
        gate_up_rows = [lax.dynamic_slice_in_dim(w, core * half_rows, half_rows, 1) for w in (w_gate, w_up)]
        gate_up_piece = jnp.concatenate(
            [dot(w[expert], choose).astype(BF16) for w in gate_up_rows for expert in range(experts)], axis=1
        )
    down_piece = lax.dynamic_slice_in_dim(w_down, hidden_at + core * own_hidden, own_hidden, 1)
    down_piece = down_piece.reshape(experts * own_hidden, width)
    if heads_spread:
        out_piece = lax.dynamic_slice_in_dim(w_out, chip * head_size + core * (head_size // 2), head_size // 2, 0)
    else:
        out_piece = lax.dynamic_slice_in_dim(w_out, core * half_rows, half_rows, 0)

    starts = jnp.cumsum(counts) - counts
    chip_of = chip ^ jnp.arange(chips, dtype=jnp.int32)
    in_block = (chip_of[:, None] * piece + jnp.arange(piece, dtype=jnp.int32)[None, :]).reshape(1, rows_here)
    positions = (starts[:, None] + in_block).reshape(group_rows)
    live = (in_block < counts[:, None]).reshape(group_rows)
    live_own = live.astype(F32).reshape(shards, chips, piece)[:, 0].reshape(rows_here, 1)
    half_size = head_size // 2
    frequency = THETA ** (-jnp.arange(half_size, dtype=F32) * 2.0 / head_size)
    phases = positions.astype(F32)[:, None] * frequency[None, :]
    cosine, sine = jnp.cos(phases), jnp.sin(phases)
    angles = (
        jnp.concatenate([cosine, cosine], axis=1),
        jnp.concatenate([-sine, sine], axis=1),
        positions[:, None],
        jnp.where(live, positions, FAR)[None, :],
    )

    with jax.named_scope("norm_in"):
        inv_in, unit_in = norm_stats(inputs)
        normed_own = (unit_in * gain_in).astype(BF16)
        normed_own, cotangent_parts = tie(normed_own, cotangent_parts)
    with jax.named_scope("rehome_cotangent"):
        extended = rehome_planes(cotangent_parts)
    with jax.named_scope("gather_normed"):
        normed = gather_first(normed_own)
        normed = gather_last(normed)
        *normed, qkv_w, out_piece, extended = tie(*normed, qkv_w, out_piece, extended)
    with jax.named_scope("weights_out"):
        out_w = from_owners(out_piece)
    with jax.named_scope("gather_upstream"):
        own_routes = extended[:, width : width + top]
        upstream_own = extended[:, :width].astype(F32) * live_own
        upstream = gather_first(jnp.concatenate([upstream_own.astype(BF16), extended[:, width:]], axis=1))
    with jax.named_scope("qkv"):
        lin, squares = run_project(normed, qkv_w, wide)
        inv_qk = lax.rsqrt(sum_rows(jnp.stack([squares[0], squares[8]], axis=0)) / width + EPS).T
        *upstream, inv_qk, out_w, gate_up_piece = tie(*upstream, inv_qk, out_w, gate_up_piece)
        upstream = gather_last(upstream)
    with jax.named_scope("weights_gate_up"):
        gate_up_w = from_owners(gate_up_piece)
    pick = (jnp.arange(HEADS, dtype=jnp.int32)[None, :] == jnp.stack(head_ids)[:, None]).astype(F32)

    def head_gain(gain):
        spread = gain.reshape(1, HEADS, head_size) * pick[:, :, None]
        return jnp.sum(spread, axis=1).reshape(1, wide)

    gains = (head_gain(gain_query), head_gain(gain_key))
    attention = (chips, heads, head_size, rows_here)
    mixed, *kept = run_attend_forward(lin, inv_qk, gains, angles, *attention)
    if not heads_spread:
        out_w = jnp.concatenate([lax.dynamic_slice_in_dim(out_w, h * head_size, head_size, 0) for h in head_ids], axis=0)
    with jax.named_scope("out_proj"):
        out_split = split_matmul(mixed, out_w, False, 6)
        upstream_full = jnp.concatenate(upstream, axis=0)
        upstream_full, *out_split = tie(upstream_full, *out_split)
        residual = inputs + scatter_chips(tuple(out_split))

    with jax.named_scope("gather_middle"):
        inv_mid, unit_mid = norm_stats(residual)
        middle_own = (unit_mid * gain_mid).astype(BF16)
        middle_own, gate_up_w, down_piece = tie(middle_own, gate_up_w, down_piece)
        middle = gather_last(gather_first(middle_own))
    with jax.named_scope("weights_down"):
        down_w = from_owners(down_piece).reshape(parts, experts, own_hidden, width)
        if not fast:
            down_w = down_w.transpose(1, 0, 2, 3).reshape(1, experts, parts * own_hidden, width)
    with jax.named_scope("router"):
        logits = dot_nt(router[:experts], middle_own)
        router_expo = jnp.exp(logits - jnp.max(logits, axis=0, keepdims=True))
        router_probs = router_expo / jnp.sum(router_expo, axis=0, keepdims=True)
        expert_ids = jnp.arange(experts, dtype=F32)
        chosen = jnp.sum(
            (own_routes.astype(F32).T[None, :, :] == expert_ids[:, None, None]).astype(F32), axis=1
        )
    with jax.named_scope("experts"):
        act, lin_grad, mix_grad = run_experts(middle, upstream, gate_up_w, down_w, router, experts, top)
        middle_split = split_matmul(lin_grad, gate_up_w, True, 14)

    with jax.named_scope("middle_grad"):
        *middle_split, mix_grad, act = tie(*middle_split, mix_grad, act)
        middle_first = scatter_first(tuple(middle_split))
        mix_grad_own = mix_grad[:rows_here].T
        for step in range(1, chips):
            part = mix_grad[step * rows_here : (step + 1) * rows_here].T
            mix_grad_own = mix_grad_own + swap(part, "chip", step)
        mix_grad_own = mix_grad_own[:experts]
    with jax.named_scope("w_down_grad"):
        if fast:
            down_total = run_down_grad(act, upstream_full, width, experts, parts)
        else:
            down_total = dot_tn(act, upstream_full[:, :width]).astype(BF16)
            down_total = down_total.reshape(experts, parts, own_hidden, width).transpose(1, 0, 2, 3)
        down_total = down_total.reshape(parts * experts * own_hidden, width)
        down_part = to_owners(down_total)
    with jax.named_scope("w_gate_up_grad"):
        gate_up_total = run_weight_grad(middle, lin_grad, 14)
    with jax.named_scope("middle_grad"):
        passed = scatter_pass(middle_first)
        *passed, gate_up_total = tie(*passed, gate_up_total)
        arrived = scatter_second(tuple(passed))
        prob_grad = mix_grad_own * chosen
        logit_grad = (router_probs * (prob_grad - jnp.sum(router_probs * prob_grad, axis=0, keepdims=True))).astype(BF16)
        middle_grad = scatter_sum(middle_first, arrived) + dot_tn(logit_grad, router[:experts])
        resid_part, gain_mid_grad = norm_back(middle_grad, unit_mid, inv_mid, gain_mid)
        resid_grad = upstream_own + resid_part
        branch_own = resid_grad.astype(BF16)
    with jax.named_scope("gather_branch"):
        branch_own, down_part, gate_up_total = tie(branch_own, down_part, gate_up_total)
        gate_up_part = to_owners(gate_up_total)
        branch = gather_first(branch_own)
    with jax.named_scope("output"):
        act, branch[0] = tie(act, branch[0])
        sum_split = split_matmul(act, down_w, False, 8)
    with jax.named_scope("mixed_grad"):
        branch = gather_last(branch)
        branch, sum_split = tie_lists(branch, sum_split)
        mixed_grad = run_back(branch, out_w, min(wide, 256))
        sum_first = scatter_first(tuple(sum_split))
    query_back, key_back, value_back, gain_grads, row_sums = run_attend_backward(
        mixed_grad, lin, kept, inv_qk, gains, angles, *attention
    )

    with jax.named_scope("qk_back"):
        *sum_first, row_sums = tie(*sum_first, row_sums)
        sum_first = tuple(sum_first)
        means = (sum_rows(jnp.stack([row_sums[0], row_sums[8]], axis=0)) / width).T
    with jax.named_scope("w_out_grad"):
        out_total = run_out_grad(mixed, branch)
        if not heads_spread:
            spread = jnp.zeros((width, width), BF16)
            for i, head in enumerate(head_ids):
                spread = lax.dynamic_update_slice_in_dim(
                    spread, out_total[i * head_size : (i + 1) * head_size], head * head_size, 0
                )
            out_total = spread
    with jax.named_scope("qk_back"):
        passed = scatter_pass(sum_first)
        *passed, means, out_total, gate_up_part = tie(*passed, means, out_total, gate_up_part)
        out_part = to_owners(out_total)
        arrived = scatter_second(tuple(passed))
        qkv_grad = run_finish((query_back, key_back, value_back), lin, gains, inv_qk, means, rows_here)
    with jax.named_scope("output"):
        expert_sum = scatter_sum(sum_first, arrived)
        output_low = ((residual + expert_sum) * live_own).astype(BF16)
    with jax.named_scope("normed_grad"):
        normed_split = split_matmul(qkv_grad, qkv_w, True, 11)
        *normed_split, output_low, qkv_grad = tie(*normed_split, output_low, qkv_grad)
        normed_first = scatter_first(tuple(normed_split))
    with jax.named_scope("w_qkv_grad"):
        qkv_total = run_weight_grad(normed, qkv_grad, 13)
    with jax.named_scope("normed_grad"):
        passed = scatter_pass(normed_first)
        *passed, qkv_total, out_part = tie(*passed, qkv_total, out_part)
        qkv_part = to_owners(qkv_total)
        arrived = scatter_second(tuple(passed))
        normed_grad = scatter_sum(normed_first, arrived)
        input_part, gain_in_grad = norm_back(normed_grad, unit_in, inv_in, gain_in)
        input_low = (resid_grad + input_part).astype(BF16)
    with jax.named_scope("input_grad"):
        input_parts = home_planes(input_low)

    if fast:
        with jax.named_scope("plane_gathers"):
            wide_first = gather_first(jnp.concatenate([gate_up_part, down_part, out_part], axis=0))
            wide_first, (input_parts, output_low) = tie_lists(wide_first, (input_parts, output_low))
            wide_last = gather_last(wide_first)
    with jax.named_scope("output"):
        output_parts = home_planes(output_low)
    with jax.named_scope("small_grads"):
        router_grad = dot(logit_grad, middle_own)

        def spread_heads(which):
            by_head = gain_grads[8 * which].reshape(heads, 1, head_size) * pick[:, :, None]
            return jnp.sum(by_head, axis=0).reshape(1, width)

        small_grads = jnp.concatenate(
            [gain_in_grad[None], spread_heads(0), spread_heads(1), gain_mid_grad[None], router_grad], axis=0
        )
        by_owner = small_grads.reshape(small_grads.shape[0], shards, shard_rows).transpose(1, 0, 2)
        small_sum = sum_chips(jnp.sum(exchange(by_owner, "shard"), axis=0))
        small_sum = small_sum + swap(small_sum, "core", 1)

    def everywhere(part):
        return lax.all_gather(part, ("chip", "core"), axis=0, tiled=False).reshape((chips, 2) + part.shape)

    def plane_parts(pieces):
        own = list(pieces)
        if len(own) != chips:
            own = own[:1] + [jnp.concatenate(own[i : i + 2], axis=0) for i in range(1, len(own), 2)]
        return own + [swap(v, "core", 1) for v in own]

    def shapes(count, *shape):
        return [jax.ShapeDtypeStruct(shape, F32)] * count

    if fast:
        with jax.named_scope("plane_gathers"):
            wide_last, (input_parts, small_sum) = tie_lists(wide_last, (input_parts, small_sum))
            qkv_first = gather_first(qkv_part)
            wide_parts = plane_parts(wide_last)
        input_grad = home_chips(input_parts)
        with jax.named_scope("w_down_grad"):
            (w_down_grad,) = place(
                functools.partial(place_rows, chips), where, wide_parts,
                (((own_hidden, width), lambda i, where: (half_rows // own_hidden + i, 0)),),
                shapes(1, experts, shard_hidden, width),
                ((1, shard_hidden, width), lambda i, where: (i, 0, 0)),
                (experts,), "place_down",
            )
        with jax.named_scope("w_out_grad"):
            out_at = half_rows + experts * own_hidden
            (w_out_grad,) = place(
                functools.partial(place_rows, chips), where, wide_parts,
                (((head_size // 2, width // 4), lambda i, where: (out_at // (head_size // 2), i)),),
                shapes(1, 1, shard_rows, width),
                ((1, shard_rows, width // 4), lambda i, where: (0, 0, i)),
                (4,), "place_out",
            )
            w_out_grad = w_out_grad.reshape(shard_rows, width)
        with jax.named_scope("w_gate_up_grad"):
            columns = jnp.concatenate([wanted + 2 * own_hidden * ((chip ^ step) - chip) for step in range(chips)])
            order = (columns[:, None] == jnp.arange(hidden, dtype=jnp.int32)[None, :]).astype(BF16)
            tile = parts * own_hidden
            w_gate_grad, w_up_grad = place(
                functools.partial(place_hidden, chips), where, wide_parts,
                (
                    ((half_rows, tile), lambda i, where: (0, i)),
                    ((half_rows, tile), lambda i, where: (0, experts + i)),
                ),
                shapes(2, experts, 2, half_rows, hidden),
                ((1, 2, half_rows, hidden), lambda i, where: (i, 0, 0, 0)),
                (experts,), "place_gate_up", (order,),
            )
            w_gate_grad = w_gate_grad.reshape(experts, shard_rows, hidden)
            w_up_grad = w_up_grad.reshape(experts, shard_rows, hidden)
        with jax.named_scope("w_qkv_grad"):
            tile = 64

            qkv_first, (w_down_grad, w_out_grad, w_gate_grad, w_up_grad) = tie_lists(
                qkv_first, (w_down_grad, w_out_grad, w_gate_grad, w_up_grad)
            )
            output = home_chips(output_parts)
            qkv_parts, (input_grad, output) = tie_lists(plane_parts(gather_last(qkv_first)), (input_grad, output))
            w_query_grad, w_key_grad, w_value_grad = (
                v.reshape(shard_rows, width)
                for v in place(
                    functools.partial(place_heads, chips, heads, head_size), where, qkv_parts,
                    (((tile, 3 * wide), lambda i, where: (i, 0)),),
                    shapes(3, 2, half_rows, width),
                    ((2, tile, width), lambda i, where: (0, i, 0)),
                    (half_rows // tile,), "place_heads",
                )
            )
    else:
        input_grad, output = home_chips(input_parts), home_chips(output_parts)
        spread = everywhere(down_part).reshape(chips, 2, experts, own_hidden, width)
        w_down_grad = spread.transpose(2, 0, 1, 3, 4).reshape(experts, shard_hidden, width).astype(F32)
        spread = everywhere(gate_up_part).reshape(chips, 2, half_rows, 2, experts, shards, 2 * own_hidden)
        spread = spread.transpose(3, 4, 1, 2, 5, 0, 6).reshape(2, experts, shard_rows, hidden).astype(F32)
        w_gate_grad, w_up_grad = spread[0], spread[1]
        if heads_spread:
            w_out_grad = everywhere(out_part).reshape(shard_rows, width).astype(F32)
        else:
            spread = lax.psum(out_part.astype(F32), "chip")
            w_out_grad = lax.all_gather(spread, "core", axis=0, tiled=True)

        def heads_back(part, count):
            spread = everywhere(part).reshape(chips, 2, half_rows, count, heads, head_size)
            return spread.transpose(3, 1, 2, 4, 0, 5).reshape(count, shard_rows, width).astype(F32)

        w_query_grad, w_key_grad, w_value_grad = heads_back(qkv_part, 3)
    return (
        output,
        input_grad,
        small_sum[0],
        w_query_grad,
        w_key_grad,
        w_value_grad,
        small_sum[1],
        small_sum[2],
        w_out_grad,
        small_sum[3],
        small_sum[4:].T,
        w_gate_grad,
        w_up_grad,
        w_down_grad,
    )


def solution(mesh):
    reps, shards = mesh.devices.shape
    split = Mesh(mesh.devices.reshape(reps // 2, 2, shards), ("chip", "core", "shard"))
    rows = P(("chip", "core", "shard"), None)
    first, second = P("shard", None), P(None, "shard", None)
    gain = P("shard")
    in_specs = (
        rows, rows, P(("chip", "core"), None), rows, gain, first, first, first, gain, gain, first, gain, first,
        second, second, second,
    )
    out_specs = (rows, rows, gain, first, first, first, gain, gain, first, gain, first, second, second, second)
    return jax.shard_map(body, mesh=split, in_specs=in_specs, out_specs=out_specs, check_vma=False)
```

profile of v0, /device:TPU:0, one launch (start us, length us, event | category | flops | bytes accessed | tf_op | source)
XLA Modules:
  0.0 758.6 jit_solution(1626941091969282546)
XLA Ops:
  18.9 3.1 collective-permute-start
  22.0 2.6 collective-permute-start.1
  24.6 3.9 all-to-all-start
  30.0 2.4 fusion.26
  37.7 3.8 all-to-all-done
  46.2 4.8 all-to-all-start.1
  59.0 8.9 %collective-permute-done.4 = bf16[1,64,2176]{2,1,0:T(8,128)(2,1)S(1)} collective-permute-done((bf16[1,64,2176]{2,1,0:T(8,128)(2,1)}, bf16[1,64,2176]{2,1,0:T(8,128)(2,1)S(1)}, u32[]{:S(2)}, u32[]{:S(2)}) %collective-permute-start.4) | collective-permute-done | bytes 278560 | tf_op jit(solution)/shard_map/rehome_cotangent/ppermute | solution.py:43
  69.4 33.4 %all-to-all-done.1 = bf16[4,64,2048]{2,1,0:T(8,128)(2,1)S(1)} async-done(((bf16[4,64,2048]{2,1,0:T(8,128)(2,1)}), bf16[4,64,2048]{2,1,0:T(8,128)(2,1)S(1)}, u32[]{:S(2)}, u32[]{:S(2)}) %all-to-all-start.1) | async-done | bytes 1048608 | tf_op jit(solution)/shard_map/norm_in/all_to_all | solution.py:142
  104.4 4.3 all-to-all-start.2
  108.8 2.3 fusion.90
  119.4 6.8 collective-permute-done.8.refs_3_
  131.6 7.0 collective-permute-done.6.refs_1_
  138.5 9.5 %collective-permute-done.10.refs_5_ = bf16[128,2048]{1,0:T(8,128)(2,1)} collective-permute-done((bf16[128,2048]{1,0:T(8,128)(2,1)}, bf16[128,2048]{1,0:T(8,128)(2,1)}, u32[]{:S(2)}, u32[]{:S(2)}) %collective-permute-start.10) | collective-permute-done | bytes 524320 | tf_op jit(solution)/shard_map/gather_normed/ppermute | solution.py:43
  155.5 16.6 %project.1 = (f32[1024,1536]{1,0:T(8,128)}, f32[24,1024]{1,0:T(8,128)}) custom-call(bf16[256,2048]{1,0:T(8,128)(2,1)} %fusion.14.refs_0_, bf16[128,2048]{1,0:T(8,128)(2,1)} %collective-permute-done.6.refs_1_, bf16[128,2048]{1,0:T(8,128)(2,1)} %collective-permute-done.7.refs_2_, bf16[128,2048]{1,0:T(8,128)(2,1)} %collective-permute-done.8.refs_3_, ...), custom_call_target="tpu_custom_call" | custom-call | flops 8800000000 | bytes 1024 | tf_op jit(solution)/shard_map/qkv/project/pallas_call | solution.py:159
  177.6 2.9 collective-permute-done.18
  196.1 16.7 %attend_forward.1 = (bf16[1024,512]{1,0:T(8,128)(2,1)}, bf16[1024,512]{1,0:T(8,128)(2,1)}, bf16[1024,512]{1,0:T(8,128)(2,1)}, bf16[1024,512]{1,0:T(8,128)(2,1)}, f32[1024,512]{1,0:T(8,128)}) custom-call(f32[1024,1536]{1,0:T(8,128)} %get-tuple-element.198.query_ref.key_ref.value_ref.lin, f32[1024,1536]{1,0:T(8,128)} %get-tuple-element.198.query_ref.key_ref.value_ref.lin, ...), custom_call_target="tpu_custom_call" | custom-call | flops 9349999616 | bytes 1024 | tf_op jit(solution)/shard_map/attend_forward/pallas_call | solution.py:159
  214.8 5.8 split_matmul.4
  224.4 20.2 %collective-permute-done.21 = bf16[2,256,1024]{2,1,0:T(8,128)(2,1)S(1)} collective-permute-done((bf16[2,256,1024]{2,1,0:T(8,128)(2,1)S(1)}, bf16[2,256,1024]{2,1,0:T(8,128)(2,1)S(1)}, u32[]{:S(2)}, u32[]{:S(2)}) %collective-permute-start.21) | collective-permute-done | bytes 1048608 | tf_op jit(solution)/shard_map/out_proj/ppermute | solution.py:43
  251.7 5.4 collective-permute-done.22
  260.6 3.5 all-gather.9.cloned.1.call-done.refs_14_.refs_15_.left_w.right_w
  269.7 10.7 %collective-permute-done.27.refs_3_ = bf16[128,2048]{1,0:T(8,128)(2,1)S(1)} collective-permute-done((bf16[128,2048]{1,0:T(8,128)(2,1)S(1)}, bf16[128,2048]{1,0:T(8,128)(2,1)S(1)}, u32[]{:S(2)}, u32[]{:S(2)}) %collective-permute-start.27) | collective-permute-done | bytes 524320 | tf_op jit(solution)/shard_map/gather_middle/ppermute | solution.py:43
  284.0 9.2 %collective-permute-done.25.refs_1_ = bf16[128,2048]{1,0:T(8,128)(2,1)S(1)} collective-permute-done((bf16[128,2048]{1,0:T(8,128)(2,1)S(1)}, bf16[128,2048]{1,0:T(8,128)(2,1)S(1)}, u32[]{:S(2)}, u32[]{:S(2)}) %collective-permute-start.25) | collective-permute-done | bytes 524320 | tf_op jit(solution)/shard_map/gather_middle/ppermute | solution.py:43
  293.2 10.2 %collective-permute-done.29.refs_5_ = bf16[128,2048]{1,0:T(8,128)(2,1)S(1)} collective-permute-done((bf16[128,2048]{1,0:T(8,128)(2,1)S(1)}, bf16[128,2048]{1,0:T(8,128)(2,1)S(1)}, u32[]{:S(2)}, u32[]{:S(2)}) %collective-permute-start.29) | collective-permute-done | bytes 524320 | tf_op jit(solution)/shard_map/gather_middle/ppermute | solution.py:43
  304.2 7.0 all-gather.11.cloned.1.call-done
  311.2 25.1 %experts.1 = (bf16[1024,1024]{1,0:T(8,128)(2,1)}, bf16[1024,2048]{1,0:T(8,128)(2,1)}, f32[1024,8]{1,0:T(8,128)}) custom-call(bf16[256,2048]{1,0:T(8,128)(2,1)} %multiply_convert_fusion.refs_0_, bf16[128,2048]{1,0:T(8,128)(2,1)} %copy-done.68, bf16[128,2048]{1,0:T(8,128)(2,1)} %copy-done.67, bf16[128,2048]{1,0:T(8,128)(2,1)} %copy-done.66, ...), custom_call_target="tpu_custom_call" | custom-call | flops 14300000256 | bytes 1024 | tf_op jit(solution)/shard_map/experts/experts/pallas_call | solution.py:159
  336.3 13.3 %split_matmul.5 = (f32[256,1024]{1,0:T(8,128)}, f32[256,1024]{1,0:T(8,128)}, bf16[2,256,1024]{2,1,0:T(8,128)(2,1)}, bf16[2,256,1024]{2,1,0:T(8,128)(2,1)}, bf16[...) custom-call(bf16[1024,2048]{1,0:T(8,128)(2,1)} %get-tuple-element.218.left.refs_7_, ...), custom_call_target="tpu_custom_call" | custom-call | flops 7699999744 | bytes 1024 | tf_op jit(solution)/shard_map/experts/split_matmul/pallas_call | solution.py:159
  349.6 8.5 %down_grad.1 = bf16[8,128,2048]{2,1,0:T(8,128)(2,1)} custom-call(bf16[1024,1024]{1,0:T(8,128)(2,1)} %get-tuple-element.241.act.left, bf16[1024,2176]{1,0:T(8,128)(2,1)} %constant_dynamic-update-slice_fusion.12.upstream), custom_call_target="tpu_custom_call" | custom-call | flops 4950000128 | bytes 1024 | tf_op jit(solution)/shard_map/w_down_grad/down_grad/pallas_call | solution.py:159
  364.9 15.3 %weight_grad.2 = bf16[2048,2048]{1,0:T(8,128)(2,1)} custom-call(bf16[256,2048]{1,0:T(8,128)(2,1)} %multiply_convert_fusion.refs_0_, bf16[128,2048]{1,0:T(8,128)(2,1)} %copy-done.68, bf16[128,2048]{1,0:T(8,128)(2,1)} %copy-done.67, bf16[128,2048]{1,0:T(8,128)(2,1)} %copy-done.66, bf16[128,2048]{1,0:T(8,128)(2,1)} %copy-done.69, bf16[128,2048]{1,0:T(8,128)(2,1)} %copy-done.70, ...), custom_call_target="tpu_custom_call" | custom-call | flops 7699999744 | bytes 1024 | tf_op jit(solution)/shard_map/w_gate_up_grad/weight_grad/pallas_call | solution.py:159
  380.2 4.7 collective-permute-done.32
  395.4 11.5 %collective-permute-done.36 = f32[8,256]{0,1:T(8,128)S(1)} collective-permute-done((f32[8,256]{0,1:T(8,128)S(1)}, f32[8,256]{0,1:T(8,128)S(1)}, u32[]{:S(2)}, u32[]{:S(2)}) %collective-permute-start.36) | collective-permute-done | bytes 8224 | tf_op jit(solution)/shard_map/middle_grad/ppermute | solution.py:43
  410.8 3.8 fusion.86
  420.4 10.8 %collective-permute-done.40.refs_3_ = bf16[128,2048]{1,0:T(8,128)(2,1)S(1)} collective-permute-done((bf16[128,2048]{1,0:T(8,128)(2,1)S(1)}, bf16[128,2048]{1,0:T(8,128)(2,1)S(1)}, u32[]{:S(2)}, u32[]{:S(2)}) %collective-permute-start.40) | collective-permute-done | bytes 524320 | tf_op jit(solution)/shard_map/gather_branch/ppermute | solution.py:43
  434.0 8.1 %split_matmul.6 = (f32[256,1024]{1,0:T(8,128)}, f32[256,1024]{1,0:T(8,128)}, bf16[2,256,1024]{2,1,0:T(8,128)(2,1)}, bf16[2,256,1024]{2,1,0:T(8,128)(2,1)}, bf16[...) custom-call(bf16[1024,1024]{1,0:T(8,128)(2,1)} %get-tuple-element.241.act.left, bf16[8,4,32,2048]{3,2,1,0:T(8,128)(2,1)} %bitcast.280, ...), custom_call_target="tpu_custom_call" | custom-call | flops 4400000000 | bytes 1024 | tf_op jit(solution)/shard_map/output/split_matmul/pallas_call | solution.py:159
  443.7 8.5 %collective-permute-done.42.refs_5_ = bf16[128,2048]{1,0:T(8,128)(2,1)S(1)} collective-permute-done((bf16[128,2048]{1,0:T(8,128)(2,1)S(1)}, bf16[128,2048]{1,0:T(8,128)(2,1)S(1)}, u32[]{:S(2)}, u32[]{:S(2)}) %collective-permute-start.42) | collective-permute-done | bytes 524320 | tf_op jit(solution)/shard_map/mixed_grad/ppermute | solution.py:43
  454.4 7.0 back.1.grad_ref
  461.4 7.5 out_grad.1
  468.9 19.2 %attend_backward.1 = (f32[1024,512]{1,0:T(8,128)}, f32[1024,512]{1,0:T(8,128)}, bf16[1024,512]{1,0:T(8,128)(2,1)}, f32[16,512]{1,0:T(8,128)}, f32[16,1024]{1,0:T(8,128)}) custom-call(bf16[1024,512]{1,0:T(8,128)(2,1)} %back.1.grad_ref, f32[1024,1536]{1,0:T(8,128)} %get-tuple-element.198.query_ref.key_ref.value_ref.lin, ...), custom_call_target="tpu_custom_call" | custom-call | flops 11000000512 | bytes 1024 | tf_op jit(solution)/shard_map/attend_backward/pallas_call | solution.py:159
  506.3 7.2 finish.1.left.refs_7_
  513.6 10.8 %split_matmul.7 = (f32[256,1024]{1,0:T(8,128)}, f32[256,1024]{1,0:T(8,128)}, bf16[2,256,1024]{2,1,0:T(8,128)(2,1)}, bf16[2,256,1024]{2,1,0:T(8,128)(2,1)}, bf16[...) custom-call(bf16[1024,1536]{1,0:T(8,128)(2,1)} %finish.1.left.refs_7_, ...), custom_call_target="tpu_custom_call" | custom-call | flops 6049999872 | bytes 1024 | tf_op jit(solution)/shard_map/normed_grad/split_matmul/pallas_call | solution.py:159
  529.8 12.7 %weight_grad.3 = bf16[2048,1536]{1,0:T(8,128)(2,1)} custom-call(bf16[256,2048]{1,0:T(8,128)(2,1)} %fusion.14.refs_0_, bf16[128,2048]{1,0:T(8,128)(2,1)} %collective-permute-done.6.refs_1_, bf16[128,2048]{1,0:T(8,128)(2,1)} %collective-permute-done.7.refs_2_, bf16[128,2048]{1,0:T(8,128)(2,1)} %collective-permute-done.8.refs_3_, ...), custom_call_target="tpu_custom_call" | custom-call | flops 7150000128 | bytes 1024 | tf_op jit(solution)/shard_map/w_qkv_grad/weight_grad/pallas_call | solution.py:159
  542.5 8.4 %collective-permute-done.51 = bf16[2,256,1024]{2,1,0:T(8,128)(2,1)S(1)} collective-permute-done((bf16[2,256,1024]{2,1,0:T(8,128)(2,1)}, bf16[2,256,1024]{2,1,0:T(8,128)(2,1)S(1)}, u32[]{:S(2)}, u32[]{:S(2)}) %collective-permute-start.51) | collective-permute-done | bytes 1048608 | tf_op jit(solution)/shard_map/normed_grad/ppermute | solution.py:43
  550.9 2.4 fusion.30
  553.3 2.4 fusion.31
  560.9 10.0 %collective-permute-done.60 = bf16[256,1024]{1,0:T(8,128)(2,1)S(1)} collective-permute-done((bf16[256,1024]{1,0:T(8,128)(2,1)}, bf16[256,1024]{1,0:T(8,128)(2,1)S(1)}, u32[]{:S(2)}, u32[]{:S(2)}) %collective-permute-start.60) | collective-permute-done | bytes 524320 | tf_op jit(solution)/shard_map/normed_grad/ppermute | solution.py:43
  573.6 3.2 fusion.9
  576.8 4.4 all-to-all-start.3
  585.2 3.8 collective-permute-done.56
  589.0 16.6 %collective-permute-done.57 = bf16[224,2048]{1,0:T(8,128)(2,1)} collective-permute-done((bf16[224,2048]{1,0:T(8,128)(2,1)}, bf16[224,2048]{1,0:T(8,128)(2,1)}, u32[]{:S(2)}, u32[]{:S(2)}) %collective-permute-start.57) | collective-permute-done | bytes 917536 | tf_op jit(solution)/shard_map/plane_gathers/ppermute | solution.py:43
  605.6 17.4 %all-to-all-done.3 = bf16[4,64,2048]{2,1,0:T(8,128)(2,1)} async-done(((bf16[4,64,2048]{2,1,0:T(8,128)(2,1)}), bf16[4,64,2048]{2,1,0:T(8,128)(2,1)}, u32[]{:S(2)}, u32[]{:S(2)}) %all-to-all-start.3) | async-done | bytes 1048608 | tf_op jit(solution)/shard_map/input_grad/all_to_all | solution.py:148
  625.4 3.9 collective-permute-start.65
  631.9 3.5 collective-permute-done.66
  637.0 6.2 collective-permute-done.67
  643.8 3.2 collective-permute-done.68
  649.2 2.3 constant_dynamic-update-slice_fusion.31.refs_3_.refs_11_
  663.7 4.6 all-to-all-start.5
  668.4 4.9 place_out.1
  673.2 6.6 place_down.1
  685.1 14.9 %place_gate_up.1 = (f32[4,2,256,1024]{3,2,1,0:T(8,128)}, f32[4,2,256,1024]{3,2,1,0:T(8,128)}) custom-call(s32[2]{0:T(128)} %pad_add_fusion.2.where_ref, bf16[448,2048]{1,0:T(8,128)(2,1)} %copy-done.2, bf16[448,2048]{1,0:T(8,128)(2,1)} %constant_dynamic-update-slice_fusion.27.refs_1_.refs_9_, ...), custom_call_target="tpu_custom_call" | custom-call | flops 4400000000 | bytes 1024 | tf_op jit(solution)/shard_map/w_gate_up_grad/place_gate_up/pallas_call | solution.py:610
  703.7 3.6 all-to-all-start.4
  714.9 8.5 %all-to-all-done.4 = bf16[4,64,2048]{2,1,0:T(8,128)(2,1)S(1)} async-done(((bf16[4,64,2048]{2,1,0:T(8,128)(2,1)}), bf16[4,64,2048]{2,1,0:T(8,128)(2,1)S(1)}, u32[]{:S(2)}, u32[]{:S(2)}) %all-to-all-start.4) | async-done | bytes 1048608 | tf_op jit(solution)/shard_map/all_to_all | solution.py:152
  723.4 3.5 all-to-all-start.6
  729.9 8.9 %all-to-all-done.6 = bf16[4,64,2048]{2,1,0:T(8,128)(2,1)S(1)} async-done(((bf16[4,64,2048]{2,1,0:T(8,128)(2,1)}), bf16[4,64,2048]{2,1,0:T(8,128)(2,1)S(1)}, u32[]{:S(2)}, u32[]{:S(2)}) %all-to-all-start.6) | async-done | bytes 1048608 | tf_op jit(solution)/shard_map/w_qkv_grad/all_to_all | solution.py:152
  738.8 8.9 %place_heads.1 = (f32[2,256,2048]{2,1,0:T(8,128)}, f32[2,256,2048]{2,1,0:T(8,128)}, f32[2,256,2048]{2,1,0:T(8,128)}) custom-call(s32[2]{0:T(128)} %pad_add_fusion.2.where_ref, bf16[256,1536]{1,0:T(8,128)(2,1)} %reduce-scatter.11.cloned.1.call-done.refs_0_, bf16[256,1536]{1,0:T(8,128)(2,1)} %constant_dynamic-update-slice_fusion.33.refs_1_, ...), custom_call_target="tpu_custom_call" | custom-call | flops 4400000000 | bytes 1024 | tf_op jit(solution)/shard_map/w_qkv_grad/place_heads/pallas_call | solution.py:610
  747.8 2.5 copy.200
  (502 shorter events, 213.4 us)
Async XLA Ops:
  7.2 140.7 %all-gather.5.cloned.1.call-start = ((), (), s32[]{:S(2)}) async-start(), calls=%async_computation.11 | async-start | bytes 7077888 | tf_op jit(solution)/shard_map/weights_qkv/all_gather | solution.py:661
  18.9 37.4 %collective-permute-start = (f32[1,8,512]{2,1,0:T(8,128)S(1)}, f32[1,8,512]{2,1,0:T(8,128)S(1)}, u32[]{:S(2)}, u32[]{:S(2)}) collective-permute-start(f32[1,8,512]{2,1,0:T(8,128)S(1)} %convert_bitcast_fusion.1), channel_id=1, source_target_pairs={{0,1},{1,0},{2,3},{3,2},{4,5},{5,4},{6,7},{7,6},{8,9},{9,8},{10,11... | collective-permute-start | bytes 49160 | tf_op jit(solution)/shard_map/small_gathers/ppermute | solution.py:43
  22.0 34.4 %collective-permute-start.1 = (f32[1,8,512]{2,1,0:T(8,128)S(1)}, f32[1,8,512]{2,1,0:T(8,128)}, u32[]{:S(2)}, u32[]{:S(2)}) collective-permute-start(f32[1,8,512]{2,1,0:T(8,128)S(1)} %convert_bitcast_fusion.1), channel_id=1, source_target_pairs={{0,2},{1,3},{2,0},{3,1},{4,6},{5,7},{6,4},{7,5},{8,10},{9,11},{10,... | collective-permute-start | bytes 49160 | tf_op jit(solution)/shard_map/small_gathers/ppermute | solution.py:43
  24.6 32.7 %collective-permute-start.2 = (f32[1,8,512]{2,1,0:T(8,128)S(1)}, f32[1,8,512]{2,1,0:T(8,128)S(1)}, u32[]{:S(2)}, u32[]{:S(2)}) collective-permute-start(f32[1,8,512]{2,1,0:T(8,128)S(1)} %convert_bitcast_fusion.1), channel_id=1, source_target_pairs={{0,3},{1,2},{2,1},{3,0},{4,7},{5,6},{6,5},{7,4},{8,11},{9,10},{10,... | collective-permute-start | bytes 49160 | tf_op jit(solution)/shard_map/small_gathers/ppermute | solution.py:43
  24.6 16.8 %all-to-all-start = ((bf16[4,64,2048]{2,1,0:T(8,128)(2,1)}), bf16[4,64,2048]{2,1,0:T(8,128)(2,1)S(1)}, u32[]{:S(2)}, u32[]{:S(2)}) async-start(bf16[4,64,2048]{2,1,0:T(8,128)(2,1)} %bitcast.241), calls=%async_computation | async-start | bytes 2097152 | tf_op jit(solution)/shard_map/rehome_tokens/all_to_all | solution.py:138
  28.5 102.9 %collective-permute-start.12 = (s32[1,4]{1,0:T(1,128)}, s32[1,4]{1,0:T(1,128)S(1)}, u32[]{:S(2)}, u32[]{:S(2)}) collective-permute-start(s32[1,4]{1,0:T(1,128)} %param.18), channel_id=1, source_target_pairs={{0,0},{1,8},{2,16},{3,24},{4,4},{5,12},{6,20},{7,28},{8,1},{9,9},{... | collective-permute-start | bytes 56 | tf_op jit(solution)/shard_map/small_gathers/ppermute | solution.py:693
  46.2 56.5 %all-to-all-start.1 = ((bf16[4,64,2048]{2,1,0:T(8,128)(2,1)}), bf16[4,64,2048]{2,1,0:T(8,128)(2,1)S(1)}, u32[]{:S(2)}, u32[]{:S(2)}) async-start(bf16[4,64,2048]{2,1,0:T(8,128)(2,1)} %copy-done.5), calls=%async_computation.1 | async-start | bytes 2097152 | tf_op jit(solution)/shard_map/norm_in/all_to_all | solution.py:142
  104.4 43.6 %all-to-all-start.2 = ((bf16[4,64,2176]{2,1,0:T(8,128)(2,1)}), bf16[4,64,2176]{2,1,0:T(8,128)(2,1)}, u32[]{:S(2)}, u32[]{:S(2)}) async-start(bf16[4,64,2176]{2,1,0:T(8,128)(2,1)} %constant_dynamic-update-slice_fusion.39), calls=%async_computation.2 | async-start | bytes 2228224 | tf_op jit(solution)/shard_map/rehome_cotangent/all_to_all | solution.py:142
  108.7 72.9 %all-gather.7.cloned.1.call-start = ((), (), s32[]{:S(2)}) async-start(), calls=%async_computation.12 | async-start | bytes 2359296 | tf_op jit(solution)/shard_map/weights_out/all_gather | solution.py:661
  117.7 20.8 %collective-permute-start.6 = (bf16[128,2048]{1,0:T(8,128)(2,1)}, bf16[128,2048]{1,0:T(8,128)(2,1)}, u32[]{:S(2)}, u32[]{:S(2)}) collective-permute-start(bf16[128,2048]{1,0:T(8,128)(2,1)} %get-tuple-element.364), channel_id=1, source_target_pairs={{0,8},{8,0},{16,24},{24,16},{1,9},{9,1},{17,25},{25,17},{2,10},{10... | collective-permute-start | bytes 1572872 | tf_op jit(solution)/shard_map/gather_normed/ppermute | solution.py:43
  118.4 20.1 %collective-permute-start.9 = (bf16[128,2048]{1,0:T(8,128)(2,1)}, bf16[128,2048]{1,0:T(8,128)(2,1)}, u32[]{:S(2)}, u32[]{:S(2)}) collective-permute-start(bf16[128,2048]{1,0:T(8,128)(2,1)} %get-tuple-element.363), channel_id=1, source_target_pairs={{0,16},{8,24},{16,0},{24,8},{1,17},{9,25},{17,1},{25,9},{2,18},{10... | collective-permute-start | bytes 1572872 | tf_op jit(solution)/shard_map/gather_normed/ppermute | solution.py:43
  126.2 21.8 %collective-permute-start.10 = (bf16[128,2048]{1,0:T(8,128)(2,1)}, bf16[128,2048]{1,0:T(8,128)(2,1)}, u32[]{:S(2)}, u32[]{:S(2)}) collective-permute-start(bf16[128,2048]{1,0:T(8,128)(2,1)} %collective-permute-done.8.refs_3_), channel_id=1, source_target_pairs={{0,8},{8,0},{16,24},{24,16},{1,9},{9,1},{17,25},{25,17},{2,10},{10... | collective-permute-start | bytes 1572872 | tf_op jit(solution)/shard_map/gather_normed/ppermute | solution.py:43
  127.4 20.6 %collective-permute-start.11 = (bf16[128,2048]{1,0:T(8,128)(2,1)}, bf16[128,2048]{1,0:T(8,128)(2,1)}, u32[]{:S(2)}, u32[]{:S(2)}) collective-permute-start(bf16[128,2048]{1,0:T(8,128)(2,1)} %collective-permute-done.7.refs_2_), channel_id=1, source_target_pairs={{0,16},{8,24},{16,0},{24,8},{1,17},{9,25},{17,1},{25,9},{2,18},{10... | collective-permute-start | bytes 1572872 | tf_op jit(solution)/shard_map/gather_normed/ppermute | solution.py:43
  148.9 115.1 %all-gather.9.cloned.1.call-start = ((), (), s32[]{:S(2)}) async-start(), calls=%async_computation.13 | async-start | bytes 9437184 | tf_op jit(solution)/shard_map/weights_gate_up/all_gather | solution.py:661
  151.5 30.1 %collective-permute-start.13 = (bf16[128,2176]{1,0:T(8,128)(2,1)}, bf16[128,2176]{1,0:T(8,128)(2,1)S(1)}, u32[]{:S(2)}, u32[]{:S(2)}) collective-permute-start(bf16[128,2176]{1,0:T(8,128)(2,1)} %get-tuple-element.355), channel_id=1, source_target_pairs={{0,8},{8,0},{16,24},{24,16},{1,9},{9,1},{17,25},{25,17},{2,10},{10... | collective-permute-start | bytes 1671176 | tf_op jit(solution)/shard_map/gather_upstream/ppermute | solution.py:43
  152.7 28.9 %collective-permute-start.15 = (bf16[128,2176]{1,0:T(8,128)(2,1)}, bf16[128,2176]{1,0:T(8,128)(2,1)}, u32[]{:S(2)}, u32[]{:S(2)}) collective-permute-start(bf16[128,2176]{1,0:T(8,128)(2,1)} %get-tuple-element.355), channel_id=1, source_target_pairs={{0,16},{8,24},{16,0},{24,8},{1,17},{9,25},{17,1},{25,9},{2,18},{10... | collective-permute-start | bytes 1671176 | tf_op jit(solution)/shard_map/gather_upstream/ppermute | solution.py:43
  153.4 28.2 %collective-permute-start.14 = (bf16[128,2176]{1,0:T(8,128)(2,1)}, bf16[128,2176]{1,0:T(8,128)(2,1)}, u32[]{:S(2)}, u32[]{:S(2)}) collective-permute-start(bf16[128,2176]{1,0:T(8,128)(2,1)} %get-tuple-element.354), channel_id=1, source_target_pairs={{0,8},{8,0},{16,24},{24,16},{1,9},{9,1},{17,25},{25,17},{2,10},{10... | collective-permute-start | bytes 1671176 | tf_op jit(solution)/shard_map/gather_upstream/ppermute | solution.py:43
  153.8 27.8 %collective-permute-start.16 = (bf16[128,2176]{1,0:T(8,128)(2,1)}, bf16[128,2176]{1,0:T(8,128)(2,1)}, u32[]{:S(2)}, u32[]{:S(2)}) collective-permute-start(bf16[128,2176]{1,0:T(8,128)(2,1)} %get-tuple-element.354), channel_id=1, source_target_pairs={{0,16},{8,24},{16,0},{24,8},{1,17},{9,25},{17,1},{25,9},{2,18},{10... | collective-permute-start | bytes 1671176 | tf_op jit(solution)/shard_map/gather_upstream/ppermute | solution.py:43
  181.7 129.5 %all-gather.11.cloned.1.call-start = ((), (), s32[]{:S(2)}) async-start(), calls=%async_computation.14 | async-start | bytes 4718592 | tf_op jit(solution)/shard_map/weights_down/all_gather | solution.py:661
  188.4 32.3 %collective-permute-start.19 = (bf16[128,2176]{1,0:T(8,128)(2,1)}, bf16[128,2176]{1,0:T(8,128)(2,1)S(1)}, u32[]{:S(2)}, u32[]{:S(2)}) collective-permute-start(bf16[128,2176]{1,0:T(8,128)(2,1)} %collective-permute-done.15.refs_10_), channel_id=1, source_target_pairs={{0,8},{8,0},{16,24},{24,16},{1,9},{9,1},{17,25},{25,17},{2,10},{10... | collective-permute-start | bytes 1671176 | tf_op jit(solution)/shard_map/qkv/ppermute | solution.py:43
  189.7 31.8 %collective-permute-start.20 = (bf16[128,2176]{1,0:T(8,128)(2,1)}, bf16[128,2176]{1,0:T(8,128)(2,1)S(1)}, u32[]{:S(2)}, u32[]{:S(2)}) collective-permute-start(bf16[128,2176]{1,0:T(8,128)(2,1)} %collective-permute-done.14.refs_9_), channel_id=1, source_target_pairs={{0,16},{8,24},{16,0},{24,8},{1,17},{9,25},{17,1},{25,9},{2,18},{10... | collective-permute-start | bytes 1671176 | tf_op jit(solution)/shard_map/qkv/ppermute | solution.py:43
  222.4 22.2 %collective-permute-start.21 = (bf16[2,256,1024]{2,1,0:T(8,128)(2,1)S(1)}, bf16[2,256,1024]{2,1,0:T(8,128)(2,1)S(1)}, u32[]{:S(2)}, u32[]{:S(2)}) collective-permute-start(bf16[2,256,1024]{2,1,0:T(8,128)(2,1)S(1)} %copy-done.65), channel_id=1, source_target_pairs={{0,8},{8,0},{16,24},{24,16},{1,9},{9,1},{17,25},{25,17},{2,10},{10... | collective-permute-start | bytes 3145736 | tf_op jit(solution)/shard_map/out_proj/ppermute | solution.py:43
  222.9 24.1 %collective-permute-start.23 = (bf16[2,256,1024]{2,1,0:T(8,128)(2,1)}, bf16[2,256,1024]{2,1,0:T(8,128)(2,1)S(1)}, u32[]{:S(2)}, u32[]{:S(2)}) collective-permute-start(bf16[2,256,1024]{2,1,0:T(8,128)(2,1)} %get-tuple-element.212), channel_id=1, source_target_pairs={{0,16},{8,24},{16,0},{24,8},{1,17},{9,25},{17,1},{25,9},{2,18},{10... | collective-permute-start | bytes 3145736 | tf_op jit(solution)/shard_map/out_proj/ppermute | solution.py:43
  264.1 150.6 %reduce-scatter.5.cloned.1.call-start = ((), (), s32[]{:S(2)}) async-start(), calls=%async_computation.15 | async-start | bytes 4718592 | tf_op jit(solution)/shard_map/w_down_grad/reduce_scatter | solution.py:664
  268.6 24.6 %collective-permute-start.25 = (bf16[128,2048]{1,0:T(8,128)(2,1)S(1)}, bf16[128,2048]{1,0:T(8,128)(2,1)S(1)}, u32[]{:S(2)}, u32[]{:S(2)}) collective-permute-start(bf16[128,2048]{1,0:T(8,128)(2,1)S(1)} %get-tuple-element.362), channel_id=1, source_target_pairs={{0,8},{8,0},{16,24},{24,16},{1,9},{9,1},{17,25},{25,17},{2,10},{10... | collective-permute-start | bytes 1572872 | tf_op jit(solution)/shard_map/gather_middle/ppermute | solution.py:43
  269.1 24.0 %collective-permute-start.28 = (bf16[128,2048]{1,0:T(8,128)(2,1)S(1)}, bf16[128,2048]{1,0:T(8,128)(2,1)S(1)}, u32[]{:S(2)}, u32[]{:S(2)}) collective-permute-start(bf16[128,2048]{1,0:T(8,128)(2,1)S(1)} %get-tuple-element.361), channel_id=1, source_target_pairs={{0,16},{8,24},{16,0},{24,8},{1,17},{9,25},{17,1},{25,9},{2,18},{10... | collective-permute-start | bytes 1572872 | tf_op jit(solution)/shard_map/gather_middle/ppermute | solution.py:43
  280.4 23.0 %collective-permute-start.29 = (bf16[128,2048]{1,0:T(8,128)(2,1)S(1)}, bf16[128,2048]{1,0:T(8,128)(2,1)S(1)}, u32[]{:S(2)}, u32[]{:S(2)}) collective-permute-start(bf16[128,2048]{1,0:T(8,128)(2,1)S(1)} %collective-permute-done.27.refs_3_), channel_id=1, source_target_pairs={{0,8},{8,0},{16,24},{24,16},{1,9},{9,1},{17,25},{25,17},{2,10},{10... | collective-permute-start | bytes 1572872 | tf_op jit(solution)/shard_map/gather_middle/ppermute | solution.py:43
  281.9 22.3 %collective-permute-start.30 = (bf16[128,2048]{1,0:T(8,128)(2,1)S(1)}, bf16[128,2048]{1,0:T(8,128)(2,1)}, u32[]{:S(2)}, u32[]{:S(2)}) collective-permute-start(bf16[128,2048]{1,0:T(8,128)(2,1)S(1)} %collective-permute-done.26.refs_2_), channel_id=1, source_target_pairs={{0,16},{8,24},{16,0},{24,8},{1,17},{9,25},{17,1},{25,9},{2,18},{10... | collective-permute-start | bytes 1572872 | tf_op jit(solution)/shard_map/gather_middle/ppermute | solution.py:43
  358.1 144.9 %reduce-scatter.7.cloned.1.call-start = ((), (), s32[]{:S(2)}) async-start(), calls=%async_computation.16 | async-start | bytes 9437184 | tf_op jit(solution)/shard_map/gather_branch/reduce_scatter | solution.py:664
  359.3 25.7 %collective-permute-start.32 = (bf16[2,256,1024]{2,1,0:T(8,128)(2,1)}, bf16[2,256,1024]{2,1,0:T(8,128)(2,1)}, u32[]{:S(2)}, u32[]{:S(2)}) collective-permute-start(bf16[2,256,1024]{2,1,0:T(8,128)(2,1)} %get-tuple-element.232), channel_id=1, source_target_pairs={{0,16},{8,24},{16,0},{24,8},{1,17},{9,25},{17,1},{25,9},{2,18},{10... | collective-permute-start | bytes 3145736 | tf_op jit(solution)/shard_map/middle_grad/ppermute | solution.py:43
  361.0 25.4 %collective-permute-start.31 = (bf16[2,256,1024]{2,1,0:T(8,128)(2,1)}, bf16[2,256,1024]{2,1,0:T(8,128)(2,1)}, u32[]{:S(2)}, u32[]{:S(2)}) collective-permute-start(bf16[2,256,1024]{2,1,0:T(8,128)(2,1)} %get-tuple-element.229), channel_id=1, source_target_pairs={{0,8},{8,0},{16,24},{24,16},{1,9},{9,1},{17,25},{25,17},{2,10},{10... | collective-permute-start | bytes 3145736 | tf_op jit(solution)/shard_map/middle_grad/ppermute | solution.py:43
  387.9 19.2 %collective-permute-start.33 = (bf16[256,1024]{1,0:T(8,128)(2,1)S(1)}, bf16[256,1024]{1,0:T(8,128)(2,1)S(1)}, u32[]{:S(2)}, u32[]{:S(2)}) collective-permute-start(bf16[256,1024]{1,0:T(8,128)(2,1)S(1)} %fusion.38), channel_id=1, source_target_pairs={{0,16},{8,24},{16,0},{24,8},{1,17},{9,25},{17,1},{25,9},{2,18},{10... | collective-permute-start | bytes 1572872 | tf_op jit(solution)/shard_map/middle_grad/ppermute | solution.py:43
  391.0 15.8 %collective-permute-start.36 = (f32[8,256]{0,1:T(8,128)S(1)}, f32[8,256]{0,1:T(8,128)S(1)}, u32[]{:S(2)}, u32[]{:S(2)}) collective-permute-start(f32[8,256]{0,1:T(8,128)S(1)} %get-tuple-element.369), channel_id=1, source_target_pairs={{0,16},{8,24},{16,0},{24,8},{1,17},{9,25},{17,1},{25,9},{2,18},{10... | collective-permute-start | bytes 24584 | tf_op jit(solution)/shard_map/middle_grad/ppermute | solution.py:43
  414.6 141.1 %reduce-scatter.9.cloned.1.call-start = ((), (), s32[]{:S(2)}) async-start(), calls=%async_computation.17 | async-start | bytes 2359296 | tf_op jit(solution)/shard_map/qk_back/reduce_scatter | solution.py:664
  419.1 24.6 %collective-permute-start.38 = (bf16[128,2048]{1,0:T(8,128)(2,1)S(1)}, bf16[128,2048]{1,0:T(8,128)(2,1)S(1)}, u32[]{:S(2)}, u32[]{:S(2)}) collective-permute-start(bf16[128,2048]{1,0:T(8,128)(2,1)S(1)} %get-tuple-element.360), channel_id=1, source_target_pairs={{0,8},{8,0},{16,24},{24,16},{1,9},{9,1},{17,25},{25,17},{2,10},{10... | collective-permute-start | bytes 1572872 | tf_op jit(solution)/shard_map/gather_branch/ppermute | solution.py:43
  419.6 24.1 %collective-permute-start.41 = (bf16[128,2048]{1,0:T(8,128)(2,1)S(1)}, bf16[128,2048]{1,0:T(8,128)(2,1)S(1)}, u32[]{:S(2)}, u32[]{:S(2)}) collective-permute-start(bf16[128,2048]{1,0:T(8,128)(2,1)S(1)} %get-tuple-element.359), channel_id=1, source_target_pairs={{0,16},{8,24},{16,0},{24,8},{1,17},{9,25},{17,1},{25,9},{2,18},{10... | collective-permute-start | bytes 1572872 | tf_op jit(solution)/shard_map/gather_branch/ppermute | solution.py:43
  431.2 21.1 %collective-permute-start.42 = (bf16[128,2048]{1,0:T(8,128)(2,1)S(1)}, bf16[128,2048]{1,0:T(8,128)(2,1)S(1)}, u32[]{:S(2)}, u32[]{:S(2)}) collective-permute-start(bf16[128,2048]{1,0:T(8,128)(2,1)S(1)} %collective-permute-done.40.refs_3_), channel_id=1, source_target_pairs={{0,8},{8,0},{16,24},{24,16},{1,9},{9,1},{17,25},{25,17},{2,10},{10... | collective-permute-start | bytes 1572872 | tf_op jit(solution)/shard_map/mixed_grad/ppermute | solution.py:43
  432.5 19.8 %collective-permute-start.43 = (bf16[128,2048]{1,0:T(8,128)(2,1)S(1)}, bf16[128,2048]{1,0:T(8,128)(2,1)S(1)}, u32[]{:S(2)}, u32[]{:S(2)}) collective-permute-start(bf16[128,2048]{1,0:T(8,128)(2,1)S(1)} %collective-permute-done.39.refs_2_), channel_id=1, source_target_pairs={{0,16},{8,24},{16,0},{24,8},{1,17},{9,25},{17,1},{25,9},{2,18},{10... | collective-permute-start | bytes 1572872 | tf_op jit(solution)/shard_map/mixed_grad/ppermute | solution.py:43
  452.3 35.8 %collective-permute-start.44 = (bf16[2,256,1024]{2,1,0:T(8,128)(2,1)}, bf16[2,256,1024]{2,1,0:T(8,128)(2,1)}, u32[]{:S(2)}, u32[]{:S(2)}) collective-permute-start(bf16[2,256,1024]{2,1,0:T(8,128)(2,1)} %get-tuple-element.264), channel_id=1, source_target_pairs={{0,8},{8,0},{16,24},{24,16},{1,9},{9,1},{17,25},{25,17},{2,10},{10... | collective-permute-start | bytes 3145736 | tf_op jit(solution)/shard_map/mixed_grad/ppermute | solution.py:43
  453.8 34.2 %collective-permute-start.45 = (bf16[2,256,1024]{2,1,0:T(8,128)(2,1)}, bf16[2,256,1024]{2,1,0:T(8,128)(2,1)}, u32[]{:S(2)}, u32[]{:S(2)}) collective-permute-start(bf16[2,256,1024]{2,1,0:T(8,128)(2,1)} %get-tuple-element.265), channel_id=1, source_target_pairs={{0,16},{8,24},{16,0},{24,8},{1,17},{9,25},{17,1},{25,9},{2,18},{10... | collective-permute-start | bytes 3145736 | tf_op jit(solution)/shard_map/mixed_grad/ppermute | solution.py:43
  503.0 176.9 %reduce-scatter.11.cloned.1.call-start = ((), (), s32[]{:S(2)}) async-start(), calls=%async_computation.18 | async-start | bytes 7077888 | tf_op jit(solution)/shard_map/normed_grad/reduce_scatter | solution.py:664
  503.3 21.0 %collective-permute-start.48 = (bf16[256,1024]{1,0:T(8,128)(2,1)}, bf16[256,1024]{1,0:T(8,128)(2,1)S(1)}, u32[]{:S(2)}, u32[]{:S(2)}) collective-permute-start(bf16[256,1024]{1,0:T(8,128)(2,1)} %fusion.35), channel_id=1, source_target_pairs={{0,16},{8,24},{16,0},{24,8},{1,17},{9,25},{17,1},{25,9},{2,18},{10... | collective-permute-start | bytes 1572872 | tf_op jit(solution)/shard_map/qk_back/ppermute | solution.py:43
  504.9 20.9 %collective-permute-start.49 = (bf16[256,1024]{1,0:T(8,128)(2,1)}, bf16[256,1024]{1,0:T(8,128)(2,1)S(1)}, u32[]{:S(2)}, u32[]{:S(2)}) collective-permute-start(bf16[256,1024]{1,0:T(8,128)(2,1)} %fusion.34), channel_id=1, source_target_pairs={{0,8},{8,0},{16,24},{24,16},{1,9},{9,1},{17,25},{25,17},{2,10},{10... | collective-permute-start | bytes 1572872 | tf_op jit(solution)/shard_map/qk_back/ppermute | solution.py:43
  528.6 22.3 %collective-permute-start.51 = (bf16[2,256,1024]{2,1,0:T(8,128)(2,1)}, bf16[2,256,1024]{2,1,0:T(8,128)(2,1)S(1)}, u32[]{:S(2)}, u32[]{:S(2)}) collective-permute-start(bf16[2,256,1024]{2,1,0:T(8,128)(2,1)} %get-tuple-element.289), channel_id=1, source_target_pairs={{0,16},{8,24},{16,0},{24,8},{1,17},{9,25},{17,1},{25,9},{2,18},{10... | collective-permute-start | bytes 3145736 | tf_op jit(solution)/shard_map/normed_grad/ppermute | solution.py:43
  529.3 24.0 %collective-permute-start.50 = (bf16[2,256,1024]{2,1,0:T(8,128)(2,1)}, bf16[2,256,1024]{2,1,0:T(8,128)(2,1)S(1)}, u32[]{:S(2)}, u32[]{:S(2)}) collective-permute-start(bf16[2,256,1024]{2,1,0:T(8,128)(2,1)} %get-tuple-element.287), channel_id=1, source_target_pairs={{0,8},{8,0},{16,24},{24,16},{1,9},{9,1},{17,25},{25,17},{2,10},{10... | collective-permute-start | bytes 3145736 | tf_op jit(solution)/shard_map/normed_grad/ppermute | solution.py:43
  556.4 15.8 %collective-permute-start.61 = (bf16[256,1024]{1,0:T(8,128)(2,1)}, bf16[256,1024]{1,0:T(8,128)(2,1)S(1)}, u32[]{:S(2)}, u32[]{:S(2)}) collective-permute-start(bf16[256,1024]{1,0:T(8,128)(2,1)} %fusion.30), channel_id=1, source_target_pairs={{0,8},{8,0},{16,24},{24,16},{1,9},{9,1},{17,25},{25,17},{2,10},{10... | collective-permute-start | bytes 1572872 | tf_op jit(solution)/shard_map/normed_grad/ppermute | solution.py:43
  558.2 30.8 %collective-permute-start.56 = (bf16[224,2048]{1,0:T(8,128)(2,1)}, bf16[224,2048]{1,0:T(8,128)(2,1)}, u32[]{:S(2)}, u32[]{:S(2)}) collective-permute-start(bf16[224,2048]{1,0:T(8,128)(2,1)} %slice.301), channel_id=1, source_target_pairs={{0,8},{8,0},{16,24},{24,16},{1,9},{9,1},{17,25},{25,17},{2,10},{10... | collective-permute-start | bytes 2752520 | tf_op jit(solution)/shard_map/plane_gathers/ppermute | solution.py:43
  559.5 29.5 %collective-permute-start.58 = (bf16[224,2048]{1,0:T(8,128)(2,1)}, bf16[224,2048]{1,0:T(8,128)(2,1)}, u32[]{:S(2)}, u32[]{:S(2)}) collective-permute-start(bf16[224,2048]{1,0:T(8,128)(2,1)} %slice.301), channel_id=1, source_target_pairs={{0,16},{8,24},{16,0},{24,8},{1,17},{9,25},{17,1},{25,9},{2,18},{10... | collective-permute-start | bytes 2752520 | tf_op jit(solution)/shard_map/plane_gathers/ppermute | solution.py:43
  576.8 46.2 %all-to-all-start.3 = ((bf16[4,64,2048]{2,1,0:T(8,128)(2,1)}), bf16[4,64,2048]{2,1,0:T(8,128)(2,1)}, u32[]{:S(2)}, u32[]{:S(2)}) async-start(bf16[4,64,2048]{2,1,0:T(8,128)(2,1)} %bitcast.234), calls=%async_computation.7 | async-start | bytes 2097152 | tf_op jit(solution)/shard_map/input_grad/all_to_all | solution.py:148
  583.4 22.3 %collective-permute-start.57 = (bf16[224,2048]{1,0:T(8,128)(2,1)}, bf16[224,2048]{1,0:T(8,128)(2,1)}, u32[]{:S(2)}, u32[]{:S(2)}) collective-permute-start(bf16[224,2048]{1,0:T(8,128)(2,1)} %slice.350), channel_id=1, source_target_pairs={{0,8},{8,0},{16,24},{24,16},{1,9},{9,1},{17,25},{25,17},{2,10},{10... | collective-permute-start | bytes 2752520 | tf_op jit(solution)/shard_map/plane_gathers/ppermute | solution.py:43
  584.0 21.7 %collective-permute-start.59 = (bf16[224,2048]{1,0:T(8,128)(2,1)}, bf16[224,2048]{1,0:T(8,128)(2,1)}, u32[]{:S(2)}, u32[]{:S(2)}) collective-permute-start(bf16[224,2048]{1,0:T(8,128)(2,1)} %slice.350), channel_id=1, source_target_pairs={{0,16},{8,24},{16,0},{24,8},{1,17},{9,25},{17,1},{25,9},{2,18},{10... | collective-permute-start | bytes 2752520 | tf_op jit(solution)/shard_map/plane_gathers/ppermute | solution.py:43
  623.0 25.1 %collective-permute-start.62 = (bf16[224,2048]{1,0:T(8,128)(2,1)}, bf16[224,2048]{1,0:T(8,128)(2,1)S(1)}, u32[]{:S(2)}, u32[]{:S(2)}) collective-permute-start(bf16[224,2048]{1,0:T(8,128)(2,1)} %collective-permute-done.58), channel_id=1, source_target_pairs={{0,8},{8,0},{16,24},{24,16},{1,9},{9,1},{17,25},{25,17},{2,10},{10... | collective-permute-start | bytes 2752520 | tf_op jit(solution)/shard_map/plane_gathers/ppermute | solution.py:43
  623.6 24.5 %collective-permute-start.63 = (bf16[224,2048]{1,0:T(8,128)(2,1)}, bf16[224,2048]{1,0:T(8,128)(2,1)}, u32[]{:S(2)}, u32[]{:S(2)}) collective-permute-start(bf16[224,2048]{1,0:T(8,128)(2,1)} %collective-permute-done.57), channel_id=1, source_target_pairs={{0,16},{8,24},{16,0},{24,8},{1,17},{9,25},{17,1},{25,9},{2,18},{10... | collective-permute-start | bytes 2752520 | tf_op jit(solution)/shard_map/plane_gathers/ppermute | solution.py:43
  651.5 16.8 %collective-permute-start.73 = (bf16[448,2048]{1,0:T(8,128)(2,1)}, bf16[448,2048]{1,0:T(8,128)(2,1)}, u32[]{:S(2)}, u32[]{:S(2)}) collective-permute-start(bf16[448,2048]{1,0:T(8,128)(2,1)} %constant_dynamic-update-slice_fusion.31.refs_3_.refs_11_), channel_id=1, source_target_pairs={{0,4},{4,0},{1,5},{5,1},{2,6},{6,2},{3,7},{7,3},{8,12},{12,8},{9,1... | collective-permute-start | bytes 5505032 | tf_op jit(solution)/shard_map/plane_gathers/ppermute | solution.py:43
  663.7 40.0 %all-to-all-start.5 = ((bf16[4,64,2048]{2,1,0:T(8,128)(2,1)}), bf16[4,64,2048]{2,1,0:T(8,128)(2,1)}, u32[]{:S(2)}, u32[]{:S(2)}) async-start(bf16[4,64,2048]{2,1,0:T(8,128)(2,1)} %bitcast.69), calls=%async_computation.9 | async-start | bytes 2097152 | tf_op jit(solution)/shard_map/output/all_to_all | solution.py:148
  681.0 19.0 %collective-permute-start.52 = (bf16[128,1536]{1,0:T(8,128)(2,1)S(1)}, bf16[128,1536]{1,0:T(8,128)(2,1)S(1)}, u32[]{:S(2)}, u32[]{:S(2)}) collective-permute-start(bf16[128,1536]{1,0:T(8,128)(2,1)S(1)} %get-tuple-element.366), channel_id=1, source_target_pairs={{0,8},{8,0},{16,24},{24,16},{1,9},{9,1},{17,25},{25,17},{2,10},{10... | collective-permute-start | bytes 1179656 | tf_op jit(solution)/shard_map/plane_gathers/ppermute | solution.py:43
  681.7 19.0 %collective-permute-start.54 = (bf16[128,1536]{1,0:T(8,128)(2,1)S(1)}, bf16[128,1536]{1,0:T(8,128)(2,1)S(1)}, u32[]{:S(2)}, u32[]{:S(2)}) collective-permute-start(bf16[128,1536]{1,0:T(8,128)(2,1)S(1)} %get-tuple-element.366), channel_id=1, source_target_pairs={{0,16},{8,24},{16,0},{24,8},{1,17},{9,25},{17,1},{25,9},{2,18},{10... | collective-permute-start | bytes 1179656 | tf_op jit(solution)/shard_map/plane_gathers/ppermute | solution.py:43
  682.2 18.5 %collective-permute-start.53 = (bf16[128,1536]{1,0:T(8,128)(2,1)S(1)}, bf16[128,1536]{1,0:T(8,128)(2,1)S(1)}, u32[]{:S(2)}, u32[]{:S(2)}) collective-permute-start(bf16[128,1536]{1,0:T(8,128)(2,1)S(1)} %get-tuple-element.365), channel_id=1, source_target_pairs={{0,8},{8,0},{16,24},{24,16},{1,9},{9,1},{17,25},{25,17},{2,10},{10... | collective-permute-start | bytes 1179656 | tf_op jit(solution)/shard_map/plane_gathers/ppermute | solution.py:43
  683.6 17.4 %collective-permute-start.55 = (bf16[128,1536]{1,0:T(8,128)(2,1)S(1)}, bf16[128,1536]{1,0:T(8,128)(2,1)S(1)}, u32[]{:S(2)}, u32[]{:S(2)}) collective-permute-start(bf16[128,1536]{1,0:T(8,128)(2,1)S(1)} %get-tuple-element.365), channel_id=1, source_target_pairs={{0,16},{8,24},{16,0},{24,8},{1,17},{9,25},{17,1},{25,9},{2,18},{10... | collective-permute-start | bytes 1179656 | tf_op jit(solution)/shard_map/plane_gathers/ppermute | solution.py:43
  702.4 24.5 %collective-permute-start.75 = (bf16[128,1536]{1,0:T(8,128)(2,1)S(1)}, bf16[128,1536]{1,0:T(8,128)(2,1)}, u32[]{:S(2)}, u32[]{:S(2)}) collective-permute-start(bf16[128,1536]{1,0:T(8,128)(2,1)S(1)} %collective-permute-done.53), channel_id=1, source_target_pairs={{0,16},{8,24},{16,0},{24,8},{1,17},{9,25},{17,1},{25,9},{2,18},{10... | collective-permute-start | bytes 1179656 | tf_op jit(solution)/shard_map/w_qkv_grad/ppermute | solution.py:43
  703.7 19.7 %all-to-all-start.4 = ((bf16[4,64,2048]{2,1,0:T(8,128)(2,1)}), bf16[4,64,2048]{2,1,0:T(8,128)(2,1)S(1)}, u32[]{:S(2)}, u32[]{:S(2)}) async-start(bf16[4,64,2048]{2,1,0:T(8,128)(2,1)} %all-to-all-done.3), calls=%async_computation.8 | async-start | bytes 2097152 | tf_op jit(solution)/shard_map/all_to_all | solution.py:152
  709.2 29.6 %collective-permute-start.78 = (bf16[256,1536]{1,0:T(8,128)(2,1)}, bf16[256,1536]{1,0:T(8,128)(2,1)}, u32[]{:S(2)}, u32[]{:S(2)}) collective-permute-start(bf16[256,1536]{1,0:T(8,128)(2,1)} %constant_dynamic-update-slice_fusion.35.refs_2_), channel_id=1, source_target_pairs={{0,4},{4,0},{1,5},{5,1},{2,6},{6,2},{3,7},{7,3},{8,12},{12,8},{9,1... | collective-permute-start | bytes 2359304 | tf_op jit(solution)/shard_map/w_qkv_grad/ppermute | solution.py:43
  710.7 28.1 %collective-permute-start.77 = (bf16[256,1536]{1,0:T(8,128)(2,1)}, bf16[256,1536]{1,0:T(8,128)(2,1)}, u32[]{:S(2)}, u32[]{:S(2)}) collective-permute-start(bf16[256,1536]{1,0:T(8,128)(2,1)} %constant_dynamic-update-slice_fusion.33.refs_1_), channel_id=1, source_target_pairs={{0,4},{4,0},{1,5},{5,1},{2,6},{6,2},{3,7},{7,3},{8,12},{12,8},{9,1... | collective-permute-start | bytes 2359304 | tf_op jit(solution)/shard_map/w_qkv_grad/ppermute | solution.py:43
  711.2 27.6 %collective-permute-start.76 = (bf16[256,1536]{1,0:T(8,128)(2,1)S(1)}, bf16[256,1536]{1,0:T(8,128)(2,1)}, u32[]{:S(2)}, u32[]{:S(2)}) collective-permute-start(bf16[256,1536]{1,0:T(8,128)(2,1)S(1)} %copy-done.26), channel_id=1, source_target_pairs={{0,4},{4,0},{1,5},{5,1},{2,6},{6,2},{3,7},{7,3},{8,12},{12,8},{9,1... | collective-permute-start | bytes 2359304 | tf_op jit(solution)/shard_map/w_qkv_grad/ppermute | solution.py:43
  (108 other events, 1282.2 us)
Sparse Core Ops, SparseCore 0:
  18.9 89.5 all-gather.4
  149.0 29.0 all-gather.6
  181.8 82.1 all-gather.8
  265.5 45.6 all-gather.10
  358.2 48.7 reduce-scatter.4
  414.8 88.1 reduce-scatter.6
  505.3 33.9 reduce-scatter.8
  555.9 86.4 reduce-scatter.10
where the time goes:
time: 770 us; the launch traced here: 759 us
  waiting for transfers between devices  272 us (35%)
  Pallas kernels  209 us (27%)
  starting transfers between devices  112 us (15%)
  local copies, waits for them, and re-layouts  75.7 us (10%)
  other arithmetic  52.1 us (7%)
  matrix products  20.8 us (3%)
  between operations  16.1 us (2%)
    ppermute x79, waiting for transfers between devices, swap(): return lax.ppermute(value, axis, [(i, i ^ step) for i in range(size)])  189 us
    pallas_call x14, Pallas kernels, run(): pl.pallas_call(kernel, grid=grid, in_specs=in_specs, out_specs=out_specs,...  174 us
    ppermute x79, starting transfers between devices, swap(): return lax.ppermute(value, axis, [(i, i ^ step) for i in range(size)])  80.2 us
    unnamed x195, local copies, waits for them, and re-layouts  36.6 us
    pallas_call x4, Pallas kernels, place(): pl.pallas_call(kernel, grid_spec=pltpu.PrefetchScalarGridSpec(num_scalar_...  35.3 us
    all_to_all x2, waiting for transfers between devices, rehome_planes(): lax.all_to_all(parts, 'shard', 0, 0, tiled=True).reshape(-1, parts.shape[2])  33.4 us
    dot_general x9, matrix products, dot(): return jnp.dot(left, right, preferred_element_type=F32)  17.6 us
    all_to_all x2, waiting for transfers between devices, home_planes(): return lax.all_to_all(parts, 'shard', 0, 0, tiled=True)  17.4 us
  transfers between devices with their start and end apart: 95, of which 41 were waited for; matrix products, arithmetic and copies ran while one was open for 17% of the time, Pallas kernels for 20%

commit v1 on v0

--- a/solution.py
+++ b/solution.py
@@ -332,7 +332,7 @@
 def run_down_grad(act, upstream, width, experts, parts):
     hidden, tile = act.shape[1], 512
     return run(
-        functools.partial(down_grad_kernel, experts, parts), "down_grad", 9, (width // tile,),
+        functools.partial(down_grad_kernel, experts, parts), "down_grad", 3, (width // tile,),
         [pl.BlockSpec(act.shape, lambda i: (0, 0)), pl.BlockSpec((upstream.shape[0], tile), lambda i: (0, i))],
         pl.BlockSpec((parts, hidden // parts, tile), lambda i: (0, 0, i)),
         jax.ShapeDtypeStruct((parts, hidden // parts, width), BF16),
@@ -813,7 +813,7 @@
         down_total = down_total.reshape(parts * experts * own_hidden, width)
         down_part = to_owners(down_total)
     with jax.named_scope("w_gate_up_grad"):
-        gate_up_total = run_weight_grad(middle, lin_grad, 14)
+        gate_up_total = run_weight_grad(middle, lin_grad, 4)
     with jax.named_scope("middle_grad"):
         passed = scatter_pass(middle_first)
         *passed, gate_up_total = tie(*passed, gate_up_total)
@@ -867,7 +867,7 @@
         *normed_split, output_low, qkv_grad = tie(*normed_split, output_low, qkv_grad)
         normed_first = scatter_first(tuple(normed_split))
     with jax.named_scope("w_qkv_grad"):
-        qkv_total = run_weight_grad(normed, qkv_grad, 13)
+        qkv_total = run_weight_grad(normed, qkv_grad, 4)
     with jax.named_scope("normed_grad"):
         passed = scatter_pass(normed_first)
         *passed, qkv_total, out_part = tie(*passed, qkv_total, out_part)

time: 770 us -> 769 us (level)
    unnamed x195 -> x203, local copies, waits for them, and re-layouts: 36.6 us -> 38 us
where the time goes in v1:
time: 769 us; the launch traced here: 758 us
  waiting for transfers between devices  272 us (35%)
  Pallas kernels  209 us (27%)
  starting transfers between devices  112 us (15%)
  local copies, waits for them, and re-layouts  76.9 us (10%)
  other arithmetic  52.2 us (7%)
  matrix products  19.5 us (3%)
  between operations  16.2 us (2%)
    ppermute x79, waiting for transfers between devices, swap(): return lax.ppermute(value, axis, [(i, i ^ step) for i in range(size)])  188 us
    pallas_call x14, Pallas kernels, run(): pl.pallas_call(kernel, grid=grid, in_specs=in_specs, out_specs=out_specs,...  174 us
    ppermute x79, starting transfers between devices, swap(): return lax.ppermute(value, axis, [(i, i ^ step) for i in range(size)])  79.8 us
    unnamed x203, local copies, waits for them, and re-layouts  38 us
    pallas_call x4, Pallas kernels, place(): pl.pallas_call(kernel, grid_spec=pltpu.PrefetchScalarGridSpec(num_scalar_...  35.3 us
    all_to_all x2, waiting for transfers between devices, rehome_planes(): lax.all_to_all(parts, 'shard', 0, 0, tiled=True).reshape(-1, parts.shape[2])  33.4 us
    dot_general x9, matrix products, dot(): return jnp.dot(left, right, preferred_element_type=F32)  17.6 us
    all_to_all x2, waiting for transfers between devices, home_planes(): return lax.all_to_all(parts, 'shard', 0, 0, tiled=True)  17.4 us
  transfers between devices with their start and end apart: 95, of which 41 were waited for; matrix products, arithmetic and copies ran while one was open for 17% of the time, Pallas kernels for 20%

profile of v1, /device:TPU:0, one launch (start us, length us, event | category | flops | bytes accessed | tf_op | source)
XLA Modules:
  0.0 757.6 jit_solution(2505197537159125293)
XLA Ops:
  18.9 3.1 collective-permute-start
  22.0 2.6 collective-permute-start.1
  24.6 3.9 all-to-all-start
  30.0 2.4 fusion.26
  37.7 3.8 all-to-all-done
  46.2 4.8 all-to-all-start.1
  59.0 8.9 %collective-permute-done.4 = bf16[1,64,2176]{2,1,0:T(8,128)(2,1)S(1)} collective-permute-done((bf16[1,64,2176]{2,1,0:T(8,128)(2,1)}, bf16[1,64,2176]{2,1,0:T(8,128)(2,1)S(1)}, u32[]{:S(2)}, u32[]{:S(2)}) %collective-permute-start.4) | collective-permute-done | bytes 278560 | tf_op jit(solution)/shard_map/rehome_cotangent/ppermute | solution.py:43
  69.4 33.4 %all-to-all-done.1 = bf16[4,64,2048]{2,1,0:T(8,128)(2,1)S(1)} async-done(((bf16[4,64,2048]{2,1,0:T(8,128)(2,1)}), bf16[4,64,2048]{2,1,0:T(8,128)(2,1)S(1)}, u32[]{:S(2)}, u32[]{:S(2)}) %all-to-all-start.1) | async-done | bytes 1048608 | tf_op jit(solution)/shard_map/norm_in/all_to_all | solution.py:142
  104.4 4.3 all-to-all-start.2
  108.8 2.3 fusion.90
  119.4 6.8 collective-permute-done.8.refs_3_
  131.6 7.0 collective-permute-done.6.refs_1_
  138.5 9.5 %collective-permute-done.10.refs_5_ = bf16[128,2048]{1,0:T(8,128)(2,1)} collective-permute-done((bf16[128,2048]{1,0:T(8,128)(2,1)}, bf16[128,2048]{1,0:T(8,128)(2,1)}, u32[]{:S(2)}, u32[]{:S(2)}) %collective-permute-start.10) | collective-permute-done | bytes 524320 | tf_op jit(solution)/shard_map/gather_normed/ppermute | solution.py:43
  155.6 16.6 %project.1 = (f32[1024,1536]{1,0:T(8,128)}, f32[24,1024]{1,0:T(8,128)}) custom-call(bf16[256,2048]{1,0:T(8,128)(2,1)} %fusion.14.refs_0_, bf16[128,2048]{1,0:T(8,128)(2,1)} %collective-permute-done.6.refs_1_, bf16[128,2048]{1,0:T(8,128)(2,1)} %collective-permute-done.7.refs_2_, bf16[128,2048]{1,0:T(8,128)(2,1)} %collective-permute-done.8.refs_3_, ...), custom_call_target="tpu_custom_call" | custom-call | flops 8800000000 | bytes 1024 | tf_op jit(solution)/shard_map/qkv/project/pallas_call | solution.py:159
  177.6 2.9 collective-permute-done.18
  196.1 16.7 %attend_forward.1 = (bf16[1024,512]{1,0:T(8,128)(2,1)}, bf16[1024,512]{1,0:T(8,128)(2,1)}, bf16[1024,512]{1,0:T(8,128)(2,1)}, bf16[1024,512]{1,0:T(8,128)(2,1)}, f32[1024,512]{1,0:T(8,128)}) custom-call(f32[1024,1536]{1,0:T(8,128)} %get-tuple-element.198.query_ref.key_ref.value_ref.lin, f32[1024,1536]{1,0:T(8,128)} %get-tuple-element.198.query_ref.key_ref.value_ref.lin, ...), custom_call_target="tpu_custom_call" | custom-call | flops 9349999616 | bytes 1024 | tf_op jit(solution)/shard_map/attend_forward/pallas_call | solution.py:159
  214.8 5.8 split_matmul.4
  224.4 20.2 %collective-permute-done.21 = bf16[2,256,1024]{2,1,0:T(8,128)(2,1)S(1)} collective-permute-done((bf16[2,256,1024]{2,1,0:T(8,128)(2,1)S(1)}, bf16[2,256,1024]{2,1,0:T(8,128)(2,1)S(1)}, u32[]{:S(2)}, u32[]{:S(2)}) %collective-permute-start.21) | collective-permute-done | bytes 1048608 | tf_op jit(solution)/shard_map/out_proj/ppermute | solution.py:43
  251.7 5.4 collective-permute-done.22
  261.3 2.7 all-gather.9.cloned.1.call-done.refs_14_.refs_15_.left_w.right_w
  268.5 10.7 %collective-permute-done.27.refs_3_ = bf16[128,2048]{1,0:T(8,128)(2,1)S(1)} collective-permute-done((bf16[128,2048]{1,0:T(8,128)(2,1)S(1)}, bf16[128,2048]{1,0:T(8,128)(2,1)S(1)}, u32[]{:S(2)}, u32[]{:S(2)}) %collective-permute-start.27) | collective-permute-done | bytes 524320 | tf_op jit(solution)/shard_map/gather_middle/ppermute | solution.py:43
  283.6 8.3 %collective-permute-done.25.refs_1_ = bf16[128,2048]{1,0:T(8,128)(2,1)S(1)} collective-permute-done((bf16[128,2048]{1,0:T(8,128)(2,1)S(1)}, bf16[128,2048]{1,0:T(8,128)(2,1)S(1)}, u32[]{:S(2)}, u32[]{:S(2)}) %collective-permute-start.25) | collective-permute-done | bytes 524320 | tf_op jit(solution)/shard_map/gather_middle/ppermute | solution.py:43
  292.0 10.2 %collective-permute-done.29.refs_5_ = bf16[128,2048]{1,0:T(8,128)(2,1)S(1)} collective-permute-done((bf16[128,2048]{1,0:T(8,128)(2,1)S(1)}, bf16[128,2048]{1,0:T(8,128)(2,1)S(1)}, u32[]{:S(2)}, u32[]{:S(2)}) %collective-permute-start.29) | collective-permute-done | bytes 524320 | tf_op jit(solution)/shard_map/gather_middle/ppermute | solution.py:43
  303.0 8.2 %all-gather.11.cloned.1.call-done = bf16[1024,2048]{1,0:T(8,128)(2,1)} async-done(((bf16[128,2048]{1,0:T(8,128)(2,1)}), bf16[1024,2048]{1,0:T(8,128)(2,1)}) %all-gather.11.cloned.1.call-update) | async-done | bytes 4194320 | tf_op jit(solution)/shard_map/weights_down/all_gather | solution.py:661
  311.2 25.1 %experts.1 = (bf16[1024,1024]{1,0:T(8,128)(2,1)}, bf16[1024,2048]{1,0:T(8,128)(2,1)}, f32[1024,8]{1,0:T(8,128)}) custom-call(bf16[256,2048]{1,0:T(8,128)(2,1)} %copy-done.3, bf16[128,2048]{1,0:T(8,128)(2,1)} %copy-done.37, bf16[128,2048]{1,0:T(8,128)(2,1)} %copy-done.36, bf16[128,2048]{1,0:T(8,128)(2,1)} %copy-done.35, bf16[128,2048]{1,0:T(8,128)(2,1)} %copy-done.38, ...), custom_call_target="tpu_custom_call" | custom-call | flops 14300000256 | bytes 1024 | tf_op jit(solution)/shard_map/experts/experts/pallas_call | solution.py:159
  336.3 13.4 %split_matmul.5 = (f32[256,1024]{1,0:T(8,128)}, f32[256,1024]{1,0:T(8,128)}, bf16[2,256,1024]{2,1,0:T(8,128)(2,1)}, bf16[2,256,1024]{2,1,0:T(8,128)(2,1)}, bf16[...) custom-call(bf16[1024,2048]{1,0:T(8,128)(2,1)} %get-tuple-element.218.left.refs_7_, ...), custom_call_target="tpu_custom_call" | custom-call | flops 7699999744 | bytes 1024 | tf_op jit(solution)/shard_map/experts/split_matmul/pallas_call | solution.py:159
  349.6 8.5 %down_grad.1 = bf16[8,128,2048]{2,1,0:T(8,128)(2,1)} custom-call(bf16[1024,1024]{1,0:T(8,128)(2,1)} %get-tuple-element.241.act.left, bf16[1024,2176]{1,0:T(8,128)(2,1)} %constant_dynamic-update-slice_fusion.12.upstream), custom_call_target="tpu_custom_call" | custom-call | flops 1650000000 | bytes 1024 | tf_op jit(solution)/shard_map/w_down_grad/down_grad/pallas_call | solution.py:159
  363.6 15.4 %weight_grad.2 = bf16[2048,2048]{1,0:T(8,128)(2,1)} custom-call(bf16[256,2048]{1,0:T(8,128)(2,1)} %copy-done.3, bf16[128,2048]{1,0:T(8,128)(2,1)} %copy-done.37, bf16[128,2048]{1,0:T(8,128)(2,1)} %copy-done.36, bf16[128,2048]{1,0:T(8,128)(2,1)} %copy-done.35, bf16[128,2048]{1,0:T(8,128)(2,1)} %copy-done.38, bf16[128,2048]{1,0:T(8,128)(2,1)} %copy-done.39, ...), custom_call_target="tpu_custom_call" | custom-call | flops 2200000000 | bytes 1024 | tf_op jit(solution)/shard_map/w_gate_up_grad/weight_grad/pallas_call | solution.py:159
  379.0 5.1 collective-permute-done.32
  395.5 10.3 %collective-permute-done.36 = f32[8,256]{0,1:T(8,128)S(1)} collective-permute-done((f32[8,256]{0,1:T(8,128)S(1)}, f32[8,256]{0,1:T(8,128)S(1)}, u32[]{:S(2)}, u32[]{:S(2)}) %collective-permute-start.36) | collective-permute-done | bytes 8224 | tf_op jit(solution)/shard_map/middle_grad/ppermute | solution.py:43
  410.9 3.8 fusion.86
  420.5 10.8 %collective-permute-done.40.refs_3_ = bf16[128,2048]{1,0:T(8,128)(2,1)S(1)} collective-permute-done((bf16[128,2048]{1,0:T(8,128)(2,1)S(1)}, bf16[128,2048]{1,0:T(8,128)(2,1)S(1)}, u32[]{:S(2)}, u32[]{:S(2)}) %collective-permute-start.40) | collective-permute-done | bytes 524320 | tf_op jit(solution)/shard_map/gather_branch/ppermute | solution.py:43
  433.3 8.2 %split_matmul.6 = (f32[256,1024]{1,0:T(8,128)}, f32[256,1024]{1,0:T(8,128)}, bf16[2,256,1024]{2,1,0:T(8,128)(2,1)}, bf16[2,256,1024]{2,1,0:T(8,128)(2,1)}, bf16[...) custom-call(bf16[1024,1024]{1,0:T(8,128)(2,1)} %get-tuple-element.241.act.left, bf16[8,4,32,2048]{3,2,1,0:T(8,128)(2,1)} %bitcast.280, ...), custom_call_target="tpu_custom_call" | custom-call | flops 4400000000 | bytes 1024 | tf_op jit(solution)/shard_map/output/split_matmul/pallas_call | solution.py:159
  443.1 8.4 %collective-permute-done.42.refs_5_ = bf16[128,2048]{1,0:T(8,128)(2,1)S(1)} collective-permute-done((bf16[128,2048]{1,0:T(8,128)(2,1)S(1)}, bf16[128,2048]{1,0:T(8,128)(2,1)S(1)}, u32[]{:S(2)}, u32[]{:S(2)}) %collective-permute-start.42) | collective-permute-done | bytes 524320 | tf_op jit(solution)/shard_map/mixed_grad/ppermute | solution.py:43
  454.0 7.0 back.1.grad_ref
  461.1 7.5 out_grad.1
  468.5 19.1 %attend_backward.1 = (f32[1024,512]{1,0:T(8,128)}, f32[1024,512]{1,0:T(8,128)}, bf16[1024,512]{1,0:T(8,128)(2,1)}, f32[16,512]{1,0:T(8,128)}, f32[16,1024]{1,0:T(8,128)}) custom-call(bf16[1024,512]{1,0:T(8,128)(2,1)} %back.1.grad_ref, f32[1024,1536]{1,0:T(8,128)} %get-tuple-element.198.query_ref.key_ref.value_ref.lin, ...), custom_call_target="tpu_custom_call" | custom-call | flops 11000000512 | bytes 1024 | tf_op jit(solution)/shard_map/attend_backward/pallas_call | solution.py:159
  498.6 2.3 fusion.46
  505.4 7.2 finish.1.left.refs_7_
  512.6 10.7 %split_matmul.7 = (f32[256,1024]{1,0:T(8,128)}, f32[256,1024]{1,0:T(8,128)}, bf16[2,256,1024]{2,1,0:T(8,128)(2,1)}, bf16[2,256,1024]{2,1,0:T(8,128)(2,1)}, bf16[...) custom-call(bf16[1024,1536]{1,0:T(8,128)(2,1)} %finish.1.left.refs_7_, ...), custom_call_target="tpu_custom_call" | custom-call | flops 6049999872 | bytes 1024 | tf_op jit(solution)/shard_map/normed_grad/split_matmul/pallas_call | solution.py:159
  528.8 12.7 %weight_grad.3 = bf16[2048,1536]{1,0:T(8,128)(2,1)} custom-call(bf16[256,2048]{1,0:T(8,128)(2,1)} %fusion.14.refs_0_, bf16[128,2048]{1,0:T(8,128)(2,1)} %collective-permute-done.6.refs_1_, bf16[128,2048]{1,0:T(8,128)(2,1)} %collective-permute-done.7.refs_2_, bf16[128,2048]{1,0:T(8,128)(2,1)} %collective-permute-done.8.refs_3_, ...), custom_call_target="tpu_custom_call" | custom-call | flops 2200000000 | bytes 1024 | tf_op jit(solution)/shard_map/w_qkv_grad/weight_grad/pallas_call | solution.py:159
  541.5 8.4 %collective-permute-done.51 = bf16[2,256,1024]{2,1,0:T(8,128)(2,1)S(1)} collective-permute-done((bf16[2,256,1024]{2,1,0:T(8,128)(2,1)}, bf16[2,256,1024]{2,1,0:T(8,128)(2,1)S(1)}, u32[]{:S(2)}, u32[]{:S(2)}) %collective-permute-start.51) | collective-permute-done | bytes 1048608 | tf_op jit(solution)/shard_map/normed_grad/ppermute | solution.py:43
  549.9 2.4 fusion.30
  552.3 2.4 fusion.31
  559.9 10.0 %collective-permute-done.60 = bf16[256,1024]{1,0:T(8,128)(2,1)S(1)} collective-permute-done((bf16[256,1024]{1,0:T(8,128)(2,1)}, bf16[256,1024]{1,0:T(8,128)(2,1)S(1)}, u32[]{:S(2)}, u32[]{:S(2)}) %collective-permute-start.60) | collective-permute-done | bytes 524320 | tf_op jit(solution)/shard_map/normed_grad/ppermute | solution.py:43
  572.6 3.2 fusion.9
  575.8 4.4 all-to-all-start.3
  584.2 3.9 collective-permute-done.56
  588.1 16.6 %collective-permute-done.57 = bf16[224,2048]{1,0:T(8,128)(2,1)} collective-permute-done((bf16[224,2048]{1,0:T(8,128)(2,1)}, bf16[224,2048]{1,0:T(8,128)(2,1)}, u32[]{:S(2)}, u32[]{:S(2)}) %collective-permute-start.57) | collective-permute-done | bytes 917536 | tf_op jit(solution)/shard_map/plane_gathers/ppermute | solution.py:43
  604.7 17.4 %all-to-all-done.3 = bf16[4,64,2048]{2,1,0:T(8,128)(2,1)} async-done(((bf16[4,64,2048]{2,1,0:T(8,128)(2,1)}), bf16[4,64,2048]{2,1,0:T(8,128)(2,1)}, u32[]{:S(2)}, u32[]{:S(2)}) %all-to-all-start.3) | async-done | bytes 1048608 | tf_op jit(solution)/shard_map/input_grad/all_to_all | solution.py:148
  624.4 3.9 collective-permute-start.65
  630.9 3.5 collective-permute-done.66
  636.0 6.3 collective-permute-done.67
  642.8 3.1 collective-permute-done.68
  662.7 4.6 all-to-all-start.5
  667.4 4.9 place_out.1
  672.3 6.6 place_down.1
  684.2 14.9 %place_gate_up.1 = (f32[4,2,256,1024]{3,2,1,0:T(8,128)}, f32[4,2,256,1024]{3,2,1,0:T(8,128)}) custom-call(s32[2]{0:T(128)} %pad_add_fusion.2.where_ref, bf16[448,2048]{1,0:T(8,128)(2,1)} %copy-done.2, bf16[448,2048]{1,0:T(8,128)(2,1)} %constant_dynamic-update-slice_fusion.27.refs_1_.refs_9_, ...), custom_call_target="tpu_custom_call" | custom-call | flops 4400000000 | bytes 1024 | tf_op jit(solution)/shard_map/w_gate_up_grad/place_gate_up/pallas_call | solution.py:610
  702.9 3.6 all-to-all-start.4
  714.0 8.5 %all-to-all-done.4 = bf16[4,64,2048]{2,1,0:T(8,128)(2,1)S(1)} async-done(((bf16[4,64,2048]{2,1,0:T(8,128)(2,1)}), bf16[4,64,2048]{2,1,0:T(8,128)(2,1)S(1)}, u32[]{:S(2)}, u32[]{:S(2)}) %all-to-all-start.4) | async-done | bytes 1048608 | tf_op jit(solution)/shard_map/all_to_all | solution.py:152
  722.5 3.5 all-to-all-start.6
  729.0 8.9 %all-to-all-done.6 = bf16[4,64,2048]{2,1,0:T(8,128)(2,1)S(1)} async-done(((bf16[4,64,2048]{2,1,0:T(8,128)(2,1)}), bf16[4,64,2048]{2,1,0:T(8,128)(2,1)S(1)}, u32[]{:S(2)}, u32[]{:S(2)}) %all-to-all-start.6) | async-done | bytes 1048608 | tf_op jit(solution)/shard_map/w_qkv_grad/all_to_all | solution.py:152
  737.9 8.9 %place_heads.1 = (f32[2,256,2048]{2,1,0:T(8,128)}, f32[2,256,2048]{2,1,0:T(8,128)}, f32[2,256,2048]{2,1,0:T(8,128)}) custom-call(s32[2]{0:T(128)} %pad_add_fusion.2.where_ref, bf16[256,1536]{1,0:T(8,128)(2,1)} %reduce-scatter.11.cloned.1.call-done.refs_0_, bf16[256,1536]{1,0:T(8,128)(2,1)} %constant_dynamic-update-slice_fusion.33.refs_1_, ...), custom_call_target="tpu_custom_call" | custom-call | flops 4400000000 | bytes 1024 | tf_op jit(solution)/shard_map/w_qkv_grad/place_heads/pallas_call | solution.py:610
  746.8 2.5 copy.200
  (510 shorter events, 213.6 us)
Async XLA Ops:
  7.2 140.8 %all-gather.5.cloned.1.call-start = ((), (), s32[]{:S(2)}) async-start(), calls=%async_computation.11 | async-start | bytes 7077888 | tf_op jit(solution)/shard_map/weights_qkv/all_gather | solution.py:661
  18.9 37.4 %collective-permute-start = (f32[1,8,512]{2,1,0:T(8,128)S(1)}, f32[1,8,512]{2,1,0:T(8,128)S(1)}, u32[]{:S(2)}, u32[]{:S(2)}) collective-permute-start(f32[1,8,512]{2,1,0:T(8,128)S(1)} %convert_bitcast_fusion.1), channel_id=1, source_target_pairs={{0,1},{1,0},{2,3},{3,2},{4,5},{5,4},{6,7},{7,6},{8,9},{9,8},{10,11... | collective-permute-start | bytes 49160 | tf_op jit(solution)/shard_map/small_gathers/ppermute | solution.py:43
  22.0 34.4 %collective-permute-start.1 = (f32[1,8,512]{2,1,0:T(8,128)S(1)}, f32[1,8,512]{2,1,0:T(8,128)}, u32[]{:S(2)}, u32[]{:S(2)}) collective-permute-start(f32[1,8,512]{2,1,0:T(8,128)S(1)} %convert_bitcast_fusion.1), channel_id=1, source_target_pairs={{0,2},{1,3},{2,0},{3,1},{4,6},{5,7},{6,4},{7,5},{8,10},{9,11},{10,... | collective-permute-start | bytes 49160 | tf_op jit(solution)/shard_map/small_gathers/ppermute | solution.py:43
  24.6 32.7 %collective-permute-start.2 = (f32[1,8,512]{2,1,0:T(8,128)S(1)}, f32[1,8,512]{2,1,0:T(8,128)S(1)}, u32[]{:S(2)}, u32[]{:S(2)}) collective-permute-start(f32[1,8,512]{2,1,0:T(8,128)S(1)} %convert_bitcast_fusion.1), channel_id=1, source_target_pairs={{0,3},{1,2},{2,1},{3,0},{4,7},{5,6},{6,5},{7,4},{8,11},{9,10},{10,... | collective-permute-start | bytes 49160 | tf_op jit(solution)/shard_map/small_gathers/ppermute | solution.py:43
  24.6 16.8 %all-to-all-start = ((bf16[4,64,2048]{2,1,0:T(8,128)(2,1)}), bf16[4,64,2048]{2,1,0:T(8,128)(2,1)S(1)}, u32[]{:S(2)}, u32[]{:S(2)}) async-start(bf16[4,64,2048]{2,1,0:T(8,128)(2,1)} %bitcast.241), calls=%async_computation | async-start | bytes 2097152 | tf_op jit(solution)/shard_map/rehome_tokens/all_to_all | solution.py:138
  28.5 102.9 %collective-permute-start.12 = (s32[1,4]{1,0:T(1,128)}, s32[1,4]{1,0:T(1,128)S(1)}, u32[]{:S(2)}, u32[]{:S(2)}) collective-permute-start(s32[1,4]{1,0:T(1,128)} %param.18), channel_id=1, source_target_pairs={{0,0},{1,8},{2,16},{3,24},{4,4},{5,12},{6,20},{7,28},{8,1},{9,9},{... | collective-permute-start | bytes 56 | tf_op jit(solution)/shard_map/small_gathers/ppermute | solution.py:693
  46.2 56.5 %all-to-all-start.1 = ((bf16[4,64,2048]{2,1,0:T(8,128)(2,1)}), bf16[4,64,2048]{2,1,0:T(8,128)(2,1)S(1)}, u32[]{:S(2)}, u32[]{:S(2)}) async-start(bf16[4,64,2048]{2,1,0:T(8,128)(2,1)} %copy-done.9), calls=%async_computation.1 | async-start | bytes 2097152 | tf_op jit(solution)/shard_map/norm_in/all_to_all | solution.py:142
  104.4 43.6 %all-to-all-start.2 = ((bf16[4,64,2176]{2,1,0:T(8,128)(2,1)}), bf16[4,64,2176]{2,1,0:T(8,128)(2,1)}, u32[]{:S(2)}, u32[]{:S(2)}) async-start(bf16[4,64,2176]{2,1,0:T(8,128)(2,1)} %constant_dynamic-update-slice_fusion.39), calls=%async_computation.2 | async-start | bytes 2228224 | tf_op jit(solution)/shard_map/rehome_cotangent/all_to_all | solution.py:142
  108.7 72.9 %all-gather.7.cloned.1.call-start = ((), (), s32[]{:S(2)}) async-start(), calls=%async_computation.12 | async-start | bytes 2359296 | tf_op jit(solution)/shard_map/weights_out/all_gather | solution.py:661
  117.7 20.8 %collective-permute-start.6 = (bf16[128,2048]{1,0:T(8,128)(2,1)}, bf16[128,2048]{1,0:T(8,128)(2,1)}, u32[]{:S(2)}, u32[]{:S(2)}) collective-permute-start(bf16[128,2048]{1,0:T(8,128)(2,1)} %get-tuple-element.364), channel_id=1, source_target_pairs={{0,8},{8,0},{16,24},{24,16},{1,9},{9,1},{17,25},{25,17},{2,10},{10... | collective-permute-start | bytes 1572872 | tf_op jit(solution)/shard_map/gather_normed/ppermute | solution.py:43
  118.4 20.1 %collective-permute-start.9 = (bf16[128,2048]{1,0:T(8,128)(2,1)}, bf16[128,2048]{1,0:T(8,128)(2,1)}, u32[]{:S(2)}, u32[]{:S(2)}) collective-permute-start(bf16[128,2048]{1,0:T(8,128)(2,1)} %get-tuple-element.363), channel_id=1, source_target_pairs={{0,16},{8,24},{16,0},{24,8},{1,17},{9,25},{17,1},{25,9},{2,18},{10... | collective-permute-start | bytes 1572872 | tf_op jit(solution)/shard_map/gather_normed/ppermute | solution.py:43
  126.2 21.8 %collective-permute-start.10 = (bf16[128,2048]{1,0:T(8,128)(2,1)}, bf16[128,2048]{1,0:T(8,128)(2,1)}, u32[]{:S(2)}, u32[]{:S(2)}) collective-permute-start(bf16[128,2048]{1,0:T(8,128)(2,1)} %collective-permute-done.8.refs_3_), channel_id=1, source_target_pairs={{0,8},{8,0},{16,24},{24,16},{1,9},{9,1},{17,25},{25,17},{2,10},{10... | collective-permute-start | bytes 1572872 | tf_op jit(solution)/shard_map/gather_normed/ppermute | solution.py:43
  127.4 20.6 %collective-permute-start.11 = (bf16[128,2048]{1,0:T(8,128)(2,1)}, bf16[128,2048]{1,0:T(8,128)(2,1)}, u32[]{:S(2)}, u32[]{:S(2)}) collective-permute-start(bf16[128,2048]{1,0:T(8,128)(2,1)} %collective-permute-done.7.refs_2_), channel_id=1, source_target_pairs={{0,16},{8,24},{16,0},{24,8},{1,17},{9,25},{17,1},{25,9},{2,18},{10... | collective-permute-start | bytes 1572872 | tf_op jit(solution)/shard_map/gather_normed/ppermute | solution.py:43
  148.9 115.1 %all-gather.9.cloned.1.call-start = ((), (), s32[]{:S(2)}) async-start(), calls=%async_computation.13 | async-start | bytes 9437184 | tf_op jit(solution)/shard_map/weights_gate_up/all_gather | solution.py:661
  151.5 30.1 %collective-permute-start.13 = (bf16[128,2176]{1,0:T(8,128)(2,1)}, bf16[128,2176]{1,0:T(8,128)(2,1)S(1)}, u32[]{:S(2)}, u32[]{:S(2)}) collective-permute-start(bf16[128,2176]{1,0:T(8,128)(2,1)} %get-tuple-element.355), channel_id=1, source_target_pairs={{0,8},{8,0},{16,24},{24,16},{1,9},{9,1},{17,25},{25,17},{2,10},{10... | collective-permute-start | bytes 1671176 | tf_op jit(solution)/shard_map/gather_upstream/ppermute | solution.py:43
  152.8 28.9 %collective-permute-start.15 = (bf16[128,2176]{1,0:T(8,128)(2,1)}, bf16[128,2176]{1,0:T(8,128)(2,1)}, u32[]{:S(2)}, u32[]{:S(2)}) collective-permute-start(bf16[128,2176]{1,0:T(8,128)(2,1)} %get-tuple-element.355), channel_id=1, source_target_pairs={{0,16},{8,24},{16,0},{24,8},{1,17},{9,25},{17,1},{25,9},{2,18},{10... | collective-permute-start | bytes 1671176 | tf_op jit(solution)/shard_map/gather_upstream/ppermute | solution.py:43
  153.4 28.2 %collective-permute-start.14 = (bf16[128,2176]{1,0:T(8,128)(2,1)}, bf16[128,2176]{1,0:T(8,128)(2,1)}, u32[]{:S(2)}, u32[]{:S(2)}) collective-permute-start(bf16[128,2176]{1,0:T(8,128)(2,1)} %get-tuple-element.354), channel_id=1, source_target_pairs={{0,8},{8,0},{16,24},{24,16},{1,9},{9,1},{17,25},{25,17},{2,10},{10... | collective-permute-start | bytes 1671176 | tf_op jit(solution)/shard_map/gather_upstream/ppermute | solution.py:43
  153.8 27.8 %collective-permute-start.16 = (bf16[128,2176]{1,0:T(8,128)(2,1)}, bf16[128,2176]{1,0:T(8,128)(2,1)}, u32[]{:S(2)}, u32[]{:S(2)}) collective-permute-start(bf16[128,2176]{1,0:T(8,128)(2,1)} %get-tuple-element.354), channel_id=1, source_target_pairs={{0,16},{8,24},{16,0},{24,8},{1,17},{9,25},{17,1},{25,9},{2,18},{10... | collective-permute-start | bytes 1671176 | tf_op jit(solution)/shard_map/gather_upstream/ppermute | solution.py:43
  181.7 129.5 %all-gather.11.cloned.1.call-start = ((), (), s32[]{:S(2)}) async-start(), calls=%async_computation.14 | async-start | bytes 4718592 | tf_op jit(solution)/shard_map/weights_down/all_gather | solution.py:661
  188.4 32.2 %collective-permute-start.19 = (bf16[128,2176]{1,0:T(8,128)(2,1)}, bf16[128,2176]{1,0:T(8,128)(2,1)S(1)}, u32[]{:S(2)}, u32[]{:S(2)}) collective-permute-start(bf16[128,2176]{1,0:T(8,128)(2,1)} %collective-permute-done.15.refs_10_), channel_id=1, source_target_pairs={{0,8},{8,0},{16,24},{24,16},{1,9},{9,1},{17,25},{25,17},{2,10},{10... | collective-permute-start | bytes 1671176 | tf_op jit(solution)/shard_map/qkv/ppermute | solution.py:43
  189.7 31.8 %collective-permute-start.20 = (bf16[128,2176]{1,0:T(8,128)(2,1)}, bf16[128,2176]{1,0:T(8,128)(2,1)S(1)}, u32[]{:S(2)}, u32[]{:S(2)}) collective-permute-start(bf16[128,2176]{1,0:T(8,128)(2,1)} %collective-permute-done.14.refs_9_), channel_id=1, source_target_pairs={{0,16},{8,24},{16,0},{24,8},{1,17},{9,25},{17,1},{25,9},{2,18},{10... | collective-permute-start | bytes 1671176 | tf_op jit(solution)/shard_map/qkv/ppermute | solution.py:43
  222.4 22.2 %collective-permute-start.21 = (bf16[2,256,1024]{2,1,0:T(8,128)(2,1)S(1)}, bf16[2,256,1024]{2,1,0:T(8,128)(2,1)S(1)}, u32[]{:S(2)}, u32[]{:S(2)}) collective-permute-start(bf16[2,256,1024]{2,1,0:T(8,128)(2,1)S(1)} %copy-done.74), channel_id=1, source_target_pairs={{0,8},{8,0},{16,24},{24,16},{1,9},{9,1},{17,25},{25,17},{2,10},{10... | collective-permute-start | bytes 3145736 | tf_op jit(solution)/shard_map/out_proj/ppermute | solution.py:43
  222.9 24.1 %collective-permute-start.23 = (bf16[2,256,1024]{2,1,0:T(8,128)(2,1)}, bf16[2,256,1024]{2,1,0:T(8,128)(2,1)S(1)}, u32[]{:S(2)}, u32[]{:S(2)}) collective-permute-start(bf16[2,256,1024]{2,1,0:T(8,128)(2,1)} %get-tuple-element.212), channel_id=1, source_target_pairs={{0,16},{8,24},{16,0},{24,8},{1,17},{9,25},{17,1},{25,9},{2,18},{10... | collective-permute-start | bytes 3145736 | tf_op jit(solution)/shard_map/out_proj/ppermute | solution.py:43
  264.1 150.7 %reduce-scatter.5.cloned.1.call-start = ((), (), s32[]{:S(2)}) async-start(), calls=%async_computation.15 | async-start | bytes 4718592 | tf_op jit(solution)/shard_map/w_down_grad/reduce_scatter | solution.py:664
  265.9 15.6 %collective-permute-start.26 = (bf16[128,2048]{1,0:T(8,128)(2,1)S(1)}, bf16[128,2048]{1,0:T(8,128)(2,1)S(1)}, u32[]{:S(2)}, u32[]{:S(2)}) collective-permute-start(bf16[128,2048]{1,0:T(8,128)(2,1)S(1)} %get-tuple-element.361), channel_id=1, source_target_pairs={{0,8},{8,0},{16,24},{24,16},{1,9},{9,1},{17,25},{25,17},{2,10},{10... | collective-permute-start | bytes 1572872 | tf_op jit(solution)/shard_map/gather_middle/ppermute | solution.py:43
  267.4 24.6 %collective-permute-start.25 = (bf16[128,2048]{1,0:T(8,128)(2,1)S(1)}, bf16[128,2048]{1,0:T(8,128)(2,1)S(1)}, u32[]{:S(2)}, u32[]{:S(2)}) collective-permute-start(bf16[128,2048]{1,0:T(8,128)(2,1)S(1)} %get-tuple-element.362), channel_id=1, source_target_pairs={{0,8},{8,0},{16,24},{24,16},{1,9},{9,1},{17,25},{25,17},{2,10},{10... | collective-permute-start | bytes 1572872 | tf_op jit(solution)/shard_map/gather_middle/ppermute | solution.py:43
  268.0 24.0 %collective-permute-start.28 = (bf16[128,2048]{1,0:T(8,128)(2,1)S(1)}, bf16[128,2048]{1,0:T(8,128)(2,1)S(1)}, u32[]{:S(2)}, u32[]{:S(2)}) collective-permute-start(bf16[128,2048]{1,0:T(8,128)(2,1)S(1)} %get-tuple-element.361), channel_id=1, source_target_pairs={{0,16},{8,24},{16,0},{24,8},{1,17},{9,25},{17,1},{25,9},{2,18},{10... | collective-permute-start | bytes 1572872 | tf_op jit(solution)/shard_map/gather_middle/ppermute | solution.py:43
  280.0 22.2 %collective-permute-start.29 = (bf16[128,2048]{1,0:T(8,128)(2,1)S(1)}, bf16[128,2048]{1,0:T(8,128)(2,1)S(1)}, u32[]{:S(2)}, u32[]{:S(2)}) collective-permute-start(bf16[128,2048]{1,0:T(8,128)(2,1)S(1)} %collective-permute-done.27.refs_3_), channel_id=1, source_target_pairs={{0,8},{8,0},{16,24},{24,16},{1,9},{9,1},{17,25},{25,17},{2,10},{10... | collective-permute-start | bytes 1572872 | tf_op jit(solution)/shard_map/gather_middle/ppermute | solution.py:43
  281.5 21.5 %collective-permute-start.30 = (bf16[128,2048]{1,0:T(8,128)(2,1)S(1)}, bf16[128,2048]{1,0:T(8,128)(2,1)}, u32[]{:S(2)}, u32[]{:S(2)}) collective-permute-start(bf16[128,2048]{1,0:T(8,128)(2,1)S(1)} %collective-permute-done.26.refs_2_), channel_id=1, source_target_pairs={{0,16},{8,24},{16,0},{24,8},{1,17},{9,25},{17,1},{25,9},{2,18},{10... | collective-permute-start | bytes 1572872 | tf_op jit(solution)/shard_map/gather_middle/ppermute | solution.py:43
  358.1 143.9 %reduce-scatter.7.cloned.1.call-start = ((), (), s32[]{:S(2)}) async-start(), calls=%async_computation.16 | async-start | bytes 9437184 | tf_op jit(solution)/shard_map/gather_branch/reduce_scatter | solution.py:664
  358.4 25.7 %collective-permute-start.32 = (bf16[2,256,1024]{2,1,0:T(8,128)(2,1)}, bf16[2,256,1024]{2,1,0:T(8,128)(2,1)}, u32[]{:S(2)}, u32[]{:S(2)}) collective-permute-start(bf16[2,256,1024]{2,1,0:T(8,128)(2,1)} %get-tuple-element.232), channel_id=1, source_target_pairs={{0,16},{8,24},{16,0},{24,8},{1,17},{9,25},{17,1},{25,9},{2,18},{10... | collective-permute-start | bytes 3145736 | tf_op jit(solution)/shard_map/middle_grad/ppermute | solution.py:43
  359.9 25.4 %collective-permute-start.31 = (bf16[2,256,1024]{2,1,0:T(8,128)(2,1)}, bf16[2,256,1024]{2,1,0:T(8,128)(2,1)}, u32[]{:S(2)}, u32[]{:S(2)}) collective-permute-start(bf16[2,256,1024]{2,1,0:T(8,128)(2,1)} %get-tuple-element.229), channel_id=1, source_target_pairs={{0,8},{8,0},{16,24},{24,16},{1,9},{9,1},{17,25},{25,17},{2,10},{10... | collective-permute-start | bytes 3145736 | tf_op jit(solution)/shard_map/middle_grad/ppermute | solution.py:43
  386.9 19.2 %collective-permute-start.33 = (bf16[256,1024]{1,0:T(8,128)(2,1)S(1)}, bf16[256,1024]{1,0:T(8,128)(2,1)S(1)}, u32[]{:S(2)}, u32[]{:S(2)}) collective-permute-start(bf16[256,1024]{1,0:T(8,128)(2,1)S(1)} %fusion.38), channel_id=1, source_target_pairs={{0,16},{8,24},{16,0},{24,8},{1,17},{9,25},{17,1},{25,9},{2,18},{10... | collective-permute-start | bytes 1572872 | tf_op jit(solution)/shard_map/middle_grad/ppermute | solution.py:43
  414.7 140.0 %reduce-scatter.9.cloned.1.call-start = ((), (), s32[]{:S(2)}) async-start(), calls=%async_computation.17 | async-start | bytes 2359296 | tf_op jit(solution)/shard_map/qk_back/reduce_scatter | solution.py:664
  418.2 24.9 %collective-permute-start.38 = (bf16[128,2048]{1,0:T(8,128)(2,1)S(1)}, bf16[128,2048]{1,0:T(8,128)(2,1)S(1)}, u32[]{:S(2)}, u32[]{:S(2)}) collective-permute-start(bf16[128,2048]{1,0:T(8,128)(2,1)S(1)} %get-tuple-element.360), channel_id=1, source_target_pairs={{0,8},{8,0},{16,24},{24,16},{1,9},{9,1},{17,25},{25,17},{2,10},{10... | collective-permute-start | bytes 1572872 | tf_op jit(solution)/shard_map/gather_branch/ppermute | solution.py:43
  419.0 24.1 %collective-permute-start.41 = (bf16[128,2048]{1,0:T(8,128)(2,1)S(1)}, bf16[128,2048]{1,0:T(8,128)(2,1)S(1)}, u32[]{:S(2)}, u32[]{:S(2)}) collective-permute-start(bf16[128,2048]{1,0:T(8,128)(2,1)S(1)} %get-tuple-element.359), channel_id=1, source_target_pairs={{0,16},{8,24},{16,0},{24,8},{1,17},{9,25},{17,1},{25,9},{2,18},{10... | collective-permute-start | bytes 1572872 | tf_op jit(solution)/shard_map/gather_branch/ppermute | solution.py:43
  431.3 20.2 %collective-permute-start.42 = (bf16[128,2048]{1,0:T(8,128)(2,1)S(1)}, bf16[128,2048]{1,0:T(8,128)(2,1)S(1)}, u32[]{:S(2)}, u32[]{:S(2)}) collective-permute-start(bf16[128,2048]{1,0:T(8,128)(2,1)S(1)} %collective-permute-done.40.refs_3_), channel_id=1, source_target_pairs={{0,8},{8,0},{16,24},{24,16},{1,9},{9,1},{17,25},{25,17},{2,10},{10... | collective-permute-start | bytes 1572872 | tf_op jit(solution)/shard_map/mixed_grad/ppermute | solution.py:43
  432.4 19.1 %collective-permute-start.43 = (bf16[128,2048]{1,0:T(8,128)(2,1)S(1)}, bf16[128,2048]{1,0:T(8,128)(2,1)S(1)}, u32[]{:S(2)}, u32[]{:S(2)}) collective-permute-start(bf16[128,2048]{1,0:T(8,128)(2,1)S(1)} %collective-permute-done.39.refs_2_), channel_id=1, source_target_pairs={{0,16},{8,24},{16,0},{24,8},{1,17},{9,25},{17,1},{25,9},{2,18},{10... | collective-permute-start | bytes 1572872 | tf_op jit(solution)/shard_map/mixed_grad/ppermute | solution.py:43
  451.5 36.2 %collective-permute-start.44 = (bf16[2,256,1024]{2,1,0:T(8,128)(2,1)}, bf16[2,256,1024]{2,1,0:T(8,128)(2,1)}, u32[]{:S(2)}, u32[]{:S(2)}) collective-permute-start(bf16[2,256,1024]{2,1,0:T(8,128)(2,1)} %get-tuple-element.264), channel_id=1, source_target_pairs={{0,8},{8,0},{16,24},{24,16},{1,9},{9,1},{17,25},{25,17},{2,10},{10... | collective-permute-start | bytes 3145736 | tf_op jit(solution)/shard_map/mixed_grad/ppermute | solution.py:43
  452.9 34.8 %collective-permute-start.45 = (bf16[2,256,1024]{2,1,0:T(8,128)(2,1)}, bf16[2,256,1024]{2,1,0:T(8,128)(2,1)}, u32[]{:S(2)}, u32[]{:S(2)}) collective-permute-start(bf16[2,256,1024]{2,1,0:T(8,128)(2,1)} %get-tuple-element.265), channel_id=1, source_target_pairs={{0,16},{8,24},{16,0},{24,8},{1,17},{9,25},{17,1},{25,9},{2,18},{10... | collective-permute-start | bytes 3145736 | tf_op jit(solution)/shard_map/mixed_grad/ppermute | solution.py:43
  502.0 176.9 %reduce-scatter.11.cloned.1.call-start = ((), (), s32[]{:S(2)}) async-start(), calls=%async_computation.18 | async-start | bytes 7077888 | tf_op jit(solution)/shard_map/normed_grad/reduce_scatter | solution.py:664
  502.4 21.0 %collective-permute-start.48 = (bf16[256,1024]{1,0:T(8,128)(2,1)}, bf16[256,1024]{1,0:T(8,128)(2,1)S(1)}, u32[]{:S(2)}, u32[]{:S(2)}) collective-permute-start(bf16[256,1024]{1,0:T(8,128)(2,1)} %fusion.35), channel_id=1, source_target_pairs={{0,16},{8,24},{16,0},{24,8},{1,17},{9,25},{17,1},{25,9},{2,18},{10... | collective-permute-start | bytes 1572872 | tf_op jit(solution)/shard_map/qk_back/ppermute | solution.py:43
  503.9 20.8 %collective-permute-start.49 = (bf16[256,1024]{1,0:T(8,128)(2,1)}, bf16[256,1024]{1,0:T(8,128)(2,1)S(1)}, u32[]{:S(2)}, u32[]{:S(2)}) collective-permute-start(bf16[256,1024]{1,0:T(8,128)(2,1)} %fusion.34), channel_id=1, source_target_pairs={{0,8},{8,0},{16,24},{24,16},{1,9},{9,1},{17,25},{25,17},{2,10},{10... | collective-permute-start | bytes 1572872 | tf_op jit(solution)/shard_map/qk_back/ppermute | solution.py:43
  527.6 22.3 %collective-permute-start.51 = (bf16[2,256,1024]{2,1,0:T(8,128)(2,1)}, bf16[2,256,1024]{2,1,0:T(8,128)(2,1)S(1)}, u32[]{:S(2)}, u32[]{:S(2)}) collective-permute-start(bf16[2,256,1024]{2,1,0:T(8,128)(2,1)} %get-tuple-element.289), channel_id=1, source_target_pairs={{0,16},{8,24},{16,0},{24,8},{1,17},{9,25},{17,1},{25,9},{2,18},{10... | collective-permute-start | bytes 3145736 | tf_op jit(solution)/shard_map/normed_grad/ppermute | solution.py:43
  528.3 24.0 %collective-permute-start.50 = (bf16[2,256,1024]{2,1,0:T(8,128)(2,1)}, bf16[2,256,1024]{2,1,0:T(8,128)(2,1)S(1)}, u32[]{:S(2)}, u32[]{:S(2)}) collective-permute-start(bf16[2,256,1024]{2,1,0:T(8,128)(2,1)} %get-tuple-element.287), channel_id=1, source_target_pairs={{0,8},{8,0},{16,24},{24,16},{1,9},{9,1},{17,25},{25,17},{2,10},{10... | collective-permute-start | bytes 3145736 | tf_op jit(solution)/shard_map/normed_grad/ppermute | solution.py:43
  555.4 15.8 %collective-permute-start.61 = (bf16[256,1024]{1,0:T(8,128)(2,1)}, bf16[256,1024]{1,0:T(8,128)(2,1)S(1)}, u32[]{:S(2)}, u32[]{:S(2)}) collective-permute-start(bf16[256,1024]{1,0:T(8,128)(2,1)} %fusion.30), channel_id=1, source_target_pairs={{0,8},{8,0},{16,24},{24,16},{1,9},{9,1},{17,25},{25,17},{2,10},{10... | collective-permute-start | bytes 1572872 | tf_op jit(solution)/shard_map/normed_grad/ppermute | solution.py:43
  557.2 30.9 %collective-permute-start.56 = (bf16[224,2048]{1,0:T(8,128)(2,1)}, bf16[224,2048]{1,0:T(8,128)(2,1)}, u32[]{:S(2)}, u32[]{:S(2)}) collective-permute-start(bf16[224,2048]{1,0:T(8,128)(2,1)} %slice.301), channel_id=1, source_target_pairs={{0,8},{8,0},{16,24},{24,16},{1,9},{9,1},{17,25},{25,17},{2,10},{10... | collective-permute-start | bytes 2752520 | tf_op jit(solution)/shard_map/plane_gathers/ppermute | solution.py:43
  558.5 29.6 %collective-permute-start.58 = (bf16[224,2048]{1,0:T(8,128)(2,1)}, bf16[224,2048]{1,0:T(8,128)(2,1)}, u32[]{:S(2)}, u32[]{:S(2)}) collective-permute-start(bf16[224,2048]{1,0:T(8,128)(2,1)} %slice.301), channel_id=1, source_target_pairs={{0,16},{8,24},{16,0},{24,8},{1,17},{9,25},{17,1},{25,9},{2,18},{10... | collective-permute-start | bytes 2752520 | tf_op jit(solution)/shard_map/plane_gathers/ppermute | solution.py:43
  575.8 46.3 %all-to-all-start.3 = ((bf16[4,64,2048]{2,1,0:T(8,128)(2,1)}), bf16[4,64,2048]{2,1,0:T(8,128)(2,1)}, u32[]{:S(2)}, u32[]{:S(2)}) async-start(bf16[4,64,2048]{2,1,0:T(8,128)(2,1)} %bitcast.234), calls=%async_computation.7 | async-start | bytes 2097152 | tf_op jit(solution)/shard_map/input_grad/all_to_all | solution.py:148
  582.4 22.3 %collective-permute-start.57 = (bf16[224,2048]{1,0:T(8,128)(2,1)}, bf16[224,2048]{1,0:T(8,128)(2,1)}, u32[]{:S(2)}, u32[]{:S(2)}) collective-permute-start(bf16[224,2048]{1,0:T(8,128)(2,1)} %slice.350), channel_id=1, source_target_pairs={{0,8},{8,0},{16,24},{24,16},{1,9},{9,1},{17,25},{25,17},{2,10},{10... | collective-permute-start | bytes 2752520 | tf_op jit(solution)/shard_map/plane_gathers/ppermute | solution.py:43
  583.0 21.7 %collective-permute-start.59 = (bf16[224,2048]{1,0:T(8,128)(2,1)}, bf16[224,2048]{1,0:T(8,128)(2,1)}, u32[]{:S(2)}, u32[]{:S(2)}) collective-permute-start(bf16[224,2048]{1,0:T(8,128)(2,1)} %slice.350), channel_id=1, source_target_pairs={{0,16},{8,24},{16,0},{24,8},{1,17},{9,25},{17,1},{25,9},{2,18},{10... | collective-permute-start | bytes 2752520 | tf_op jit(solution)/shard_map/plane_gathers/ppermute | solution.py:43
  622.1 25.1 %collective-permute-start.62 = (bf16[224,2048]{1,0:T(8,128)(2,1)}, bf16[224,2048]{1,0:T(8,128)(2,1)S(1)}, u32[]{:S(2)}, u32[]{:S(2)}) collective-permute-start(bf16[224,2048]{1,0:T(8,128)(2,1)} %collective-permute-done.58), channel_id=1, source_target_pairs={{0,8},{8,0},{16,24},{24,16},{1,9},{9,1},{17,25},{25,17},{2,10},{10... | collective-permute-start | bytes 2752520 | tf_op jit(solution)/shard_map/plane_gathers/ppermute | solution.py:43
  622.7 24.5 %collective-permute-start.63 = (bf16[224,2048]{1,0:T(8,128)(2,1)}, bf16[224,2048]{1,0:T(8,128)(2,1)}, u32[]{:S(2)}, u32[]{:S(2)}) collective-permute-start(bf16[224,2048]{1,0:T(8,128)(2,1)} %collective-permute-done.57), channel_id=1, source_target_pairs={{0,16},{8,24},{16,0},{24,8},{1,17},{9,25},{17,1},{25,9},{2,18},{10... | collective-permute-start | bytes 2752520 | tf_op jit(solution)/shard_map/plane_gathers/ppermute | solution.py:43
  650.5 16.9 %collective-permute-start.73 = (bf16[448,2048]{1,0:T(8,128)(2,1)}, bf16[448,2048]{1,0:T(8,128)(2,1)}, u32[]{:S(2)}, u32[]{:S(2)}) collective-permute-start(bf16[448,2048]{1,0:T(8,128)(2,1)} %constant_dynamic-update-slice_fusion.31.refs_3_.refs_11_), channel_id=1, source_target_pairs={{0,4},{4,0},{1,5},{5,1},{2,6},{6,2},{3,7},{7,3},{8,12},{12,8},{9,1... | collective-permute-start | bytes 5505032 | tf_op jit(solution)/shard_map/plane_gathers/ppermute | solution.py:43
  662.7 40.1 %all-to-all-start.5 = ((bf16[4,64,2048]{2,1,0:T(8,128)(2,1)}), bf16[4,64,2048]{2,1,0:T(8,128)(2,1)}, u32[]{:S(2)}, u32[]{:S(2)}) async-start(bf16[4,64,2048]{2,1,0:T(8,128)(2,1)} %bitcast.69), calls=%async_computation.9 | async-start | bytes 2097152 | tf_op jit(solution)/shard_map/output/all_to_all | solution.py:148
  680.1 19.0 %collective-permute-start.52 = (bf16[128,1536]{1,0:T(8,128)(2,1)S(1)}, bf16[128,1536]{1,0:T(8,128)(2,1)S(1)}, u32[]{:S(2)}, u32[]{:S(2)}) collective-permute-start(bf16[128,1536]{1,0:T(8,128)(2,1)S(1)} %get-tuple-element.366), channel_id=1, source_target_pairs={{0,8},{8,0},{16,24},{24,16},{1,9},{9,1},{17,25},{25,17},{2,10},{10... | collective-permute-start | bytes 1179656 | tf_op jit(solution)/shard_map/plane_gathers/ppermute | solution.py:43
  680.7 19.0 %collective-permute-start.54 = (bf16[128,1536]{1,0:T(8,128)(2,1)S(1)}, bf16[128,1536]{1,0:T(8,128)(2,1)S(1)}, u32[]{:S(2)}, u32[]{:S(2)}) collective-permute-start(bf16[128,1536]{1,0:T(8,128)(2,1)S(1)} %get-tuple-element.366), channel_id=1, source_target_pairs={{0,16},{8,24},{16,0},{24,8},{1,17},{9,25},{17,1},{25,9},{2,18},{10... | collective-permute-start | bytes 1179656 | tf_op jit(solution)/shard_map/plane_gathers/ppermute | solution.py:43
  681.3 18.4 %collective-permute-start.53 = (bf16[128,1536]{1,0:T(8,128)(2,1)S(1)}, bf16[128,1536]{1,0:T(8,128)(2,1)S(1)}, u32[]{:S(2)}, u32[]{:S(2)}) collective-permute-start(bf16[128,1536]{1,0:T(8,128)(2,1)S(1)} %get-tuple-element.365), channel_id=1, source_target_pairs={{0,8},{8,0},{16,24},{24,16},{1,9},{9,1},{17,25},{25,17},{2,10},{10... | collective-permute-start | bytes 1179656 | tf_op jit(solution)/shard_map/plane_gathers/ppermute | solution.py:43
  682.7 17.3 %collective-permute-start.55 = (bf16[128,1536]{1,0:T(8,128)(2,1)S(1)}, bf16[128,1536]{1,0:T(8,128)(2,1)S(1)}, u32[]{:S(2)}, u32[]{:S(2)}) collective-permute-start(bf16[128,1536]{1,0:T(8,128)(2,1)S(1)} %get-tuple-element.365), channel_id=1, source_target_pairs={{0,16},{8,24},{16,0},{24,8},{1,17},{9,25},{17,1},{25,9},{2,18},{10... | collective-permute-start | bytes 1179656 | tf_op jit(solution)/shard_map/plane_gathers/ppermute | solution.py:43
  701.5 24.5 %collective-permute-start.75 = (bf16[128,1536]{1,0:T(8,128)(2,1)S(1)}, bf16[128,1536]{1,0:T(8,128)(2,1)}, u32[]{:S(2)}, u32[]{:S(2)}) collective-permute-start(bf16[128,1536]{1,0:T(8,128)(2,1)S(1)} %collective-permute-done.53), channel_id=1, source_target_pairs={{0,16},{8,24},{16,0},{24,8},{1,17},{9,25},{17,1},{25,9},{2,18},{10... | collective-permute-start | bytes 1179656 | tf_op jit(solution)/shard_map/w_qkv_grad/ppermute | solution.py:43
  702.9 19.6 %all-to-all-start.4 = ((bf16[4,64,2048]{2,1,0:T(8,128)(2,1)}), bf16[4,64,2048]{2,1,0:T(8,128)(2,1)S(1)}, u32[]{:S(2)}, u32[]{:S(2)}) async-start(bf16[4,64,2048]{2,1,0:T(8,128)(2,1)} %all-to-all-done.3), calls=%async_computation.8 | async-start | bytes 2097152 | tf_op jit(solution)/shard_map/all_to_all | solution.py:152
  708.3 29.5 %collective-permute-start.78 = (bf16[256,1536]{1,0:T(8,128)(2,1)}, bf16[256,1536]{1,0:T(8,128)(2,1)}, u32[]{:S(2)}, u32[]{:S(2)}) collective-permute-start(bf16[256,1536]{1,0:T(8,128)(2,1)} %constant_dynamic-update-slice_fusion.35.refs_2_), channel_id=1, source_target_pairs={{0,4},{4,0},{1,5},{5,1},{2,6},{6,2},{3,7},{7,3},{8,12},{12,8},{9,1... | collective-permute-start | bytes 2359304 | tf_op jit(solution)/shard_map/w_qkv_grad/ppermute | solution.py:43
  709.8 28.0 %collective-permute-start.77 = (bf16[256,1536]{1,0:T(8,128)(2,1)}, bf16[256,1536]{1,0:T(8,128)(2,1)}, u32[]{:S(2)}, u32[]{:S(2)}) collective-permute-start(bf16[256,1536]{1,0:T(8,128)(2,1)} %constant_dynamic-update-slice_fusion.33.refs_1_), channel_id=1, source_target_pairs={{0,4},{4,0},{1,5},{5,1},{2,6},{6,2},{3,7},{7,3},{8,12},{12,8},{9,1... | collective-permute-start | bytes 2359304 | tf_op jit(solution)/shard_map/w_qkv_grad/ppermute | solution.py:43
  710.4 27.5 %collective-permute-start.76 = (bf16[256,1536]{1,0:T(8,128)(2,1)S(1)}, bf16[256,1536]{1,0:T(8,128)(2,1)}, u32[]{:S(2)}, u32[]{:S(2)}) collective-permute-start(bf16[256,1536]{1,0:T(8,128)(2,1)S(1)} %copy-done.30), channel_id=1, source_target_pairs={{0,4},{4,0},{1,5},{5,1},{2,6},{6,2},{3,7},{7,3},{8,12},{12,8},{9,1... | collective-permute-start | bytes 2359304 | tf_op jit(solution)/shard_map/w_qkv_grad/ppermute | solution.py:43
  (112 other events, 1343.5 us)
Sparse Core Ops, SparseCore 0:
  18.9 89.5 all-gather.4
  149.0 29.0 all-gather.6
  181.8 82.1 all-gather.8
  265.5 45.6 all-gather.10
  358.3 48.7 reduce-scatter.4
  414.9 87.1 reduce-scatter.6
  504.3 33.9 reduce-scatter.8
  554.9 86.5 reduce-scatter.10
